TPU v7x, 32 devices: a whole 2x2x4 slice. The times are simulated.
32 devices in a mesh: parts: 2 (over y), ctx: 4 (over z), head: 2 (over x), sub: 2 (over core).
Axes of the slice: x: 2, y: 2, z: 4, core: 2. Of those that a mesh axis runs over, the one named last changes fastest.
Arguments:
- queries: bfloat16 [1024, 12288], P(('parts', 'ctx'), ('head', 'sub')), parts along dimension 0, may hold values from -250 to 250
- latent: bfloat16 [1024, 512], P(('parts', 'ctx')), parts along dimension 0, may hold values from -6 to 6
- rope_keys: bfloat16 [1024, 64], P(('parts', 'ctx')), parts along dimension 0, may hold values from -4 to 4
- latent_gain: float32 [512], replicated, may hold values from 0.1 to 1.9
- up_weight: bfloat16 [512, 16384], P(None, ('head', 'sub')), may hold values from -0.25 to 0.25
- prompt_length: int32 [2], P('parts'), parts along dimension 0, may hold values from 256 to 512
Outputs:
- attended: bfloat16 [1024, 8192], P(('parts', 'ctx'), ('head', 'sub')), parts along dimension 0
There are 2 independent parts, one for each index of `parts`. A program takes and returns all parts, laid end to end along the dimension named above; an argument that names none is the same for every part. Nothing has to cross between parts.
All inputs are finite; a program needn't handle non-finite values.
Results may differ from a plain program's by a relative error of at most 0.012.
Values may be sent and summed in bfloat16 or wider, within the bound.
A program may use at most 128 MiB of HBM per device.

v0:
```python
import math

import jax
import jax.numpy as jnp
from jax import lax
from jax.sharding import PartitionSpec as P

ROPE = 64
NOPE = 128
VDIM = 128


def rotate(values, positions):
    half_width = values.shape[-1] // 2
    frequency = 10000.0 ** (-jnp.arange(half_width, dtype=jnp.float32) / half_width)
    angles = positions.astype(jnp.float32)[..., None] * frequency
    cosines = jnp.cos(angles)
    sines = jnp.sin(angles)
    lower_half = values[..., :half_width]
    upper_half = values[..., half_width:]
    return jnp.concatenate(
        [lower_half * cosines - upper_half * sines, lower_half * sines + upper_half * cosines], -1
    )


def attend(carried, keys_values, rope_piece, query_nope, query_rope, query_pos, length):
    running_max, running_sum, weighted = carried
    key_count = keys_values.shape[0]
    heads_dev = query_nope.shape[1]
    grouped = keys_values.reshape(key_count, heads_dev, NOPE + VDIM)
    scores = jnp.einsum(
        "qhd,khd->hqk", query_nope, grouped[:, :, :NOPE], preferred_element_type=jnp.float32
    )
    scores = scores + jnp.einsum(
        "qhr,kr->hqk", query_rope, rope_piece, preferred_element_type=jnp.float32
    )
    scores = scores * (1.0 / math.sqrt(NOPE + ROPE))
    key_pos = jnp.arange(key_count, dtype=jnp.int32)
    allowed = (key_pos[None, :] <= query_pos[:, None]) & (key_pos[None, :] < length)
    scores = jnp.where(allowed[None], scores, -1e30)
    new_max = jnp.maximum(running_max, jnp.max(scores, -1))
    weights = jnp.where(allowed[None], jnp.exp(scores - new_max[:, :, None]), 0.0)
    running_sum = jnp.sum(weights, -1)
    weighted = jnp.einsum(
        "hqk,khv->hqv",
        weights.astype(jnp.bfloat16),
        grouped[:, :, NOPE:],
        preferred_element_type=jnp.float32,
    )
    return (new_max, running_sum, weighted)


def per_device(queries, latent, rope_keys, latent_gain, up_weight, prompt_length):
    length = prompt_length[0]
    latent_rows = latent.shape[0]
    latent_start = lax.axis_index("ctx") * latent_rows
    latent_pos = latent_start + jnp.arange(latent_rows, dtype=jnp.int32)
    widened = latent.astype(jnp.float32)
    shard_latent = (
        widened * lax.rsqrt(jnp.mean(widened * widened, -1, keepdims=True) + 1e-06) * latent_gain
    ).astype(jnp.bfloat16)
    shard_rope = rotate(rope_keys.astype(jnp.float32), latent_pos).astype(jnp.bfloat16)
    token_rows = queries.shape[0]
    heads_dev = up_weight.shape[1] // (NOPE + VDIM)
    query_start = lax.axis_index("ctx") * token_rows
    query_pos = query_start + jnp.arange(token_rows, dtype=jnp.int32)
    grouped = queries.reshape(token_rows, heads_dev, NOPE + ROPE)
    query_nope = grouped[:, :, :NOPE]
    query_rope = rotate(grouped[:, :, NOPE:].astype(jnp.float32), query_pos[:, None]).astype(
        jnp.bfloat16
    )
    start_state = (
        jnp.full((heads_dev, token_rows), -1e30, jnp.float32),
        jnp.zeros((heads_dev, token_rows), jnp.float32),
        jnp.zeros((heads_dev, token_rows, VDIM), jnp.float32),
    )
    keys_values = jnp.dot(
        lax.all_gather(shard_latent, "ctx", axis=0, tiled=True),
        up_weight,
        preferred_element_type=jnp.float32,
    ).astype(jnp.bfloat16)
    rope_piece = lax.all_gather(shard_rope, "ctx", axis=0, tiled=True)
    running_max, running_sum, weighted = attend(
        start_state, keys_values, rope_piece, query_nope, query_rope, query_pos, length
    )
    result = weighted / running_sum[:, :, None]
    result = jnp.where(query_pos[None, :, None] < length, result, 0.0)
    return result.astype(jnp.bfloat16).transpose(1, 0, 2).reshape(token_rows, heads_dev * VDIM)


def solution(mesh):
    placed = (
        P(("parts", "ctx"), ("head", "sub")),
        P(("parts", "ctx"), None),
        P(("parts", "ctx"), None),
        P(),
        P(None, ("head", "sub")),
        P("parts"),
    )
    return jax.shard_map(
        per_device,
        mesh=mesh,
        in_specs=placed,
        out_specs=P(("parts", "ctx"), ("head", "sub")),
        check_vma=False,
    )
```

profile of v0, /device:TPU:0, one launch (start us, length us, event | category | flops | bytes accessed | tf_op | source)
XLA Modules:
  0.0 46.7 jit_solution(16228726584107372220)
XLA Ops:
  0.0 1.5 %copy.15 = bf16[128,3072]{0,1:T(8,128)(2,1)S(1)} copy(bf16[128,3072]{1,0:T(8,128)(2,1)} %param.6) | data formatting | bytes 1572864 | tf_op args[0]
  1.6 0.7 %convert_element_type.41 = f32[128,64]{0,1:T(8,128)S(1)} convert(bf16[128,64]{0,1:T(8,128)(2,1)} %param.8) | non-fusion elementwise | flops 8192 | bytes 49152 | tf_op jit(solution)/shard_map/convert_element_type | solution.py:62
  2.3 0.1 subtract_convert_fusion.1
  2.5 0.1 subtract_convert_fusion
  2.6 13.7 %all_gather.7 = bf16[512,64]{0,1:T(8,128)(2,1)S(1)} all-gather(bf16[128,64]{0,1:T(8,128)(2,1)S(1)} %pad_maximum_fusion), channel_id=1, replica_groups=mesh['parts'=2,'ctx'=4,'head'=2,'sub'=2] {'ctx'}, dimensions={0}, use_global_device_ids=true | all-gather | bytes 81920 | tf_op jit(solution)/shard_map/all_gather | solution.py:82
  16.2 1.0 %fusion.22 = f32[128]{0:T(128)S(1)} fusion(bf16[128,512]{1,0:T(8,128)(2,1)} %param.7), kind=kLoop, calls=%fused_computation.19 | loop fusion | flops 196480 | bytes 131584 | tf_op jit(solution)/shard_map/reduce_sum | solution.py:60
  17.3 1.0 %fusion.24 = bf16[128,512]{1,0:T(8,128)(2,1)S(1)} fusion(bf16[128,512]{1,0:T(8,128)(2,1)} %param.7, f32[512]{0:T(512)} %param.9, f32[128]{0:T(128)S(1)} %add_rsqrt_fusion), kind=kLoop, calls=%fused_computation.21 | loop fusion | flops 262144 | bytes 264704 | tf_op jit(solution)/shard_map/convert_element_type | solution.py:61
  18.3 15.9 %all_gather.6 = bf16[512,512]{1,0:T(8,128)(2,1)S(1)} all-gather(bf16[128,512]{1,0:T(8,128)(2,1)S(1)} %fusion.24), channel_id=1, replica_groups=mesh['parts'=2,'ctx'=4,'head'=2,'sub'=2] {'ctx'}, dimensions={0}, use_global_device_ids=true | all-gather | bytes 655360 | tf_op jit(solution)/shard_map/all_gather | solution.py:78
  34.2 4.5 %convolution_convert_fusion = bf16[512,4096]{1,0:T(8,128)(2,1)S(1)} fusion(bf16[512,512]{1,0:T(8,128)(2,1)S(1)} %all_gather.6, bf16[512,4096]{1,0:T(8,128)(2,1)} %param.10), kind=kOutput, calls=%fused_computation | convolution fusion | flops 2149580800 | bytes 8912896 | tf_op jit(solution)/shard_map/dot_general | solution.py:77
  38.7 1.4 %copy.24 = bf16[64,8,16,256]{3,2,1,0:T(8,128)(2,1)S(1)} copy(bf16[64,8,16,256]{3,1,2,0:T(8,128)(2,1)S(1)} %bitcast.28) | data formatting | bytes 8388608
  40.1 0.7 %fusion.33 = (bf16[512,16,128]{2,1,0:T(8,128)(2,1)S(1)}, bf16[512,16,128]{2,1,0:T(8,128)(2,1)S(1)}) fusion(bf16[512,16,256]{2,1,0:T(8,128)(2,1)S(1)} %bitcast.27), kind=kLoop, calls=%fused_computation.45 | loop fusion | bytes 8388608 | tf_op jit(solution)/shard_map/slice | solution.py:47
  40.9 0.7 %fusion.6 = f32[16,512,128]{2,1,0:T(8,128)S(1)} fusion(bf16[512,16,128]{2,1,0:T(8,128)(2,1)S(1)} %get-tuple-element.6, bf16[128,16,192]{0,2,1:T(8,128)(2,1)S(1)} %bitcast.30), kind=kOutput, calls=%fused_computation.8 | convolution fusion | flops 268435456 | bytes 6815744 | tf_op jit(solution)/shard_map/qhd,khd->hqk/dot_general | solution.py:31
  42.2 0.1 fusion.28
  42.4 0.9 %fusion.34 = (f32[16,128]{1,0:T(8,128)S(1)}, f32[16,128,512]{1,2,0:T(8,128)S(1)}) fusion(bf16[128,16,32]{0,2,1:T(8,128)(2,1)S(1)} %get-tuple-element.8, bf16[128,16,32]{0,2,1:T(8,128)(2,1)S(1)} %get-tuple-element.7, bf16[512,64]{0,1:T(8,128)(2,1)S(1)} %all_gather.7, f32[16,512,128]{2,1,0:T(8,128)S(1)} %fusion.6, pred[128,512]{0,1:T(8,128)(4,1)S(1)} %fusion.28), kind=kOutput, calls=%fused_computation.46 | convolution fusion | flops 138934272 | bytes 8790016 | tf_op jit(solution)/shard_map/qhr,kr->hqk/dot_general | solution.py:34
  43.3 0.7 %fusion.2 = f32[16,128]{1,0:T(8,128)S(1)} fusion(f32[16,128,512]{1,2,0:T(8,128)S(1)} %get-tuple-element.14, f32[16,128]{1,0:T(8,128)S(1)} %broadcast_maximum_fusion, pred[128,512]{0,1:T(8,128)(4,1)S(1)} %fusion.28), kind=kLoop, calls=%fused_computation.5 | loop fusion | flops 3143680 | bytes 4276224 | tf_op jit(solution)/shard_map/reduce_sum | solution.py:43
  44.1 1.6 %select_convert_fusion = bf16[128,16,128]{0,2,1:T(8,128)(2,1)S(1)} fusion(f32[16,128,512]{1,2,0:T(8,128)S(1)} %get-tuple-element.14, f32[16,128]{1,0:T(8,128)S(1)} %broadcast_maximum_fusion, pred[128,512]{0,1:T(8,128)(4,1)S(1)} %fusion.28, bf16[512,16,128]{2,1,0:T(8,128)(2,1)S(1)} %get-tuple-element.5, f32[128,16]{0,1:T(8,128)S(1)} %bitcast.32, ...), kind=kOutput, calls=%fused_computation.15 | convolution fusion | flops 272367616 | bytes 6897792 | tf_op jit(solution)/shard_map/hqk,khv->hqv/dot_general | solution.py:44
  45.7 1.0 %copy.19 = bf16[128,2048]{1,0:T(8,128)(2,1)} copy(bf16[128,2048]{0,1:T(8,128)(2,1)S(1)} %bitcast.31) | data formatting | bytes 1048576 | tf_op jit(solution)/shard_map/reshape | solution.py:88
  (9 shorter events, 0.1 us)
where the time goes:
time: 47 us; the launch traced here: 46.7 us
  blocking collectives  29.6 us (63%)
  matrix products  7.79 us (17%)
  local copies, waits for them, and re-layouts  4.64 us (10%)
  other arithmetic  3.91 us (8%)
  between operations  0.79 us (2%)
    all_gather x1, blocking collectives, per_device(): lax.all_gather(shard_latent, 'ctx', axis=0, tiled=True)  15.9 us
    all_gather x1, blocking collectives, per_device(): rope_piece = lax.all_gather(shard_rope, 'ctx', axis=0, tiled=True)  13.7 us
    dot_general x1, matrix products, per_device(): jnp.dot(lax.all_gather(shard_latent, 'ctx', axis=0, tiled=True), up_weigh...  4.53 us
    unnamed x2, local copies, waits for them, and re-layouts  2.91 us
    dot_general x1, matrix products, attend(): jnp.einsum('hqk,khv->hqv', weights.astype(jnp.bfloat16), grouped[:, :, NO...  1.62 us
    reduce_sum x1, other arithmetic, per_device(): jnp.mean(widened * widened, -1, keepdims=True) + 1e-06  1.01 us
    convert_element_type x1, other arithmetic, per_device(): shard_latent = (widened * lax.rsqrt(jnp.mean(widened * widened, -1, keepd...  1.01 us
    reshape x1, local copies, waits for them, and re-layouts, per_device(): result.astype(jnp.bfloat16).transpose(1, 0, 2)  1.01 us

commit v1 on v0

v1 whole, which is shorter than its diff:
```python
import functools
import math

import jax
import jax.numpy as jnp
from jax import lax
from jax.experimental import pallas as pl
from jax.experimental.pallas import tpu as pltpu
from jax.sharding import PartitionSpec as P

ROPE = 64
NOPE = 128
VDIM = 128
QDIM = NOPE + ROPE
KVDIM = NOPE + VDIM
MESH = pl.DeviceIdType.MESH
SCORE_SCALE = math.log2(math.e) / math.sqrt(NOPE + ROPE)


def angle_tables(first_pos, rows):
    lane8 = lax.broadcasted_iota(jnp.int32, (8, 2 * ROPE), 1)
    half = ROPE // 2
    frequency = jnp.exp((lane8 % half).astype(jnp.float32) * (-math.log(10000.0) / half))
    low = lax.broadcasted_iota(jnp.int32, (8, 2 * ROPE), 0).astype(jnp.float32) * frequency
    blocks = rows // 8
    lane = lax.broadcasted_iota(jnp.int32, (blocks, 2 * ROPE), 1)
    block_frequency = jnp.exp((lane % half).astype(jnp.float32) * (-math.log(10000.0) / half))
    base = (first_pos + 8 * lax.broadcasted_iota(jnp.int32, (blocks, 2 * ROPE), 0)).astype(jnp.float32)
    high = base * block_frequency
    cos_low, sin_low = jnp.cos(low), jnp.sin(low)
    cos_high, sin_high = jnp.cos(high), jnp.sin(high)
    cosines, sines = [], []
    for block in range(blocks):
        ch, sh = cos_high[block : block + 1], sin_high[block : block + 1]
        cosines.append(ch * cos_low - sh * sin_low)
        sines.append(sh * cos_low + ch * sin_low)
    cosine = jnp.concatenate(cosines, 0)
    sine = jnp.concatenate(sines, 0)
    lane = lax.broadcasted_iota(jnp.int32, (rows, 2 * ROPE), 1)
    return cosine, jnp.where(lane % ROPE < half, -sine, sine)


def rotate_pair(values, cosine, sine):
    half = ROPE // 2
    lane = lax.broadcasted_iota(jnp.int32, values.shape, 1)
    swapped = jnp.where(
        lane % ROPE < half, pltpu.roll(values, 2 * ROPE - half, 1), pltpu.roll(values, half, 1)
    )
    return values * cosine + swapped * sine


def kernel(
    n, n_head, n_sub, chunk,
    length_ref, queries, latent, rope_keys, latent_gain, up_weight, out,
    keys, q_raw, q_ready, w_buf, lat_buf, rope_buf, gain_buf, out_buf,
    load_sem, w_sem, out_sem, z_send, z_recv, x_send, x_recv, s_send, s_recv,
):
    ctx = lax.axis_index("ctx")
    head = lax.axis_index("head")
    sub = lax.axis_index("sub")
    rows = latent.shape[0]
    width = latent.shape[1]
    pairs = w_buf.shape[0]
    pair_w = 2 * KVDIM
    pair_q = 2 * QDIM
    piece = rows // (n_head * n_sub)

    loads = [
        pltpu.make_async_copy(latent, lat_buf, load_sem.at[0]),
        pltpu.make_async_copy(rope_keys, rope_buf, load_sem.at[1]),
        pltpu.make_async_copy(latent_gain, gain_buf, load_sem.at[2]),
        pltpu.make_async_copy(queries, q_raw, load_sem.at[3]),
    ]
    for load in loads:
        load.start()

    def w_load(pair):
        return pltpu.make_async_copy(
            up_weight.at[:, pl.ds(pl.multiple_of(pair * pair_w, pair_w), pair_w)],
            w_buf.at[pair],
            w_sem.at[pair],
        )

    for pair in range(pairs):
        w_load(pair).start()

    barrier = pltpu.get_barrier_semaphore()
    for other in range(n - 1):

        @pl.when(other < ctx)
        def _():
            pl.semaphore_signal(barrier, inc=1, device_id={"ctx": other}, device_id_type=MESH)

    @pl.when(ctx > 0)
    def _():
        for step in range(1, n_head):
            pl.semaphore_signal(
                barrier, inc=1, device_id={"head": lax.rem(head + step, n_head)}, device_id_type=MESH
            )
        for step in range(1, n_sub):
            pl.semaphore_signal(
                barrier, inc=1, device_id={"sub": lax.rem(sub + step, n_sub)}, device_id_type=MESH
            )

    cosine, sine = angle_tables(ctx * rows, rows)

    loads[0].wait()
    loads[1].wait()
    loads[2].wait()
    widened = lat_buf[...].astype(jnp.float32)
    mean = jnp.mean(widened * widened, -1, keepdims=True)
    normed = (widened * lax.rsqrt(mean + 1e-06) * gain_buf[...].reshape(1, width)).astype(jnp.bfloat16)
    rope = rope_buf[...].astype(jnp.float32)
    rotated = rotate_pair(jnp.concatenate([rope, rope], 1), cosine, sine).astype(jnp.bfloat16)
    own = pl.ds(pl.multiple_of(ctx * rows, rows), rows)
    keys[own, pl.ds(0, width)] = normed
    keys[own, pl.ds(width, 2 * ROPE)] = rotated

    waits = jnp.where(ctx > 0, n_head - 1 + n_sub - 1, 0) + (n - 1 - ctx)
    pl.semaphore_wait(barrier, waits)

    def rows_of(shard, x, s):
        return pl.ds(pl.multiple_of(shard * rows + (x * n_sub + s) * piece, piece), piece)

    def z_copy(shard, target):
        where = keys.at[rows_of(shard, head, sub)]
        return pltpu.make_async_remote_copy(
            where, where, z_send.at[target], z_recv.at[shard],
            device_id={"ctx": target}, device_id_type=MESH,
        )

    def x_copy(shard, x, step):
        where = keys.at[rows_of(shard, x, sub)]
        return pltpu.make_async_remote_copy(
            where, where, x_send.at[shard, step], x_recv.at[shard, x],
            device_id={"head": lax.rem(head + step, n_head)}, device_id_type=MESH,
        )

    def s_copy(shard, x, s, step):
        where = keys.at[rows_of(shard, x, s)]
        return pltpu.make_async_remote_copy(
            where, where, s_send.at[shard, x, step], s_recv.at[shard, x, s],
            device_id={"sub": lax.rem(sub + step, n_sub)}, device_id_type=MESH,
        )

    for target in range(n - 1, 0, -1):

        @pl.when(ctx < target)
        def _():
            z_copy(ctx, target).start()

    for shard in range(1, n):

        @pl.when(ctx < shard)
        def _():
            keys[pl.ds(shard * rows, rows), :] = jnp.zeros((rows, width + 2 * ROPE), jnp.bfloat16)

    loads[3].wait()
    lane = lax.broadcasted_iota(jnp.int32, (rows, 2 * ROPE), 1)
    lower = lane < ROPE

    def ready(pair, carry):
        at = pl.multiple_of(pair * pair_q, 128)
        tile1 = q_raw[:, pl.ds(at + NOPE, 128)].astype(jnp.float32)
        tile2 = q_raw[:, pl.ds(at + 2 * NOPE, 128)].astype(jnp.float32)
        spun = rotate_pair(jnp.where(lower, tile1, tile2), cosine, sine)
        q_ready[2 * pair, :, :NOPE] = q_raw[:, pl.ds(at, NOPE)]
        q_ready[2 * pair, :, NOPE:] = jnp.where(lower, spun, 0.0).astype(jnp.bfloat16)
        q_ready[2 * pair + 1, :, :NOPE] = pltpu.roll(
            jnp.where(lower, tile2, tile1), ROPE, 1
        ).astype(jnp.bfloat16)
        q_ready[2 * pair + 1, :, NOPE:] = jnp.where(lower, 0.0, spun).astype(jnp.bfloat16)
        return carry

    lax.fori_loop(0, pairs, ready, 0)

    for shard in range(n - 2, -1, -1):

        @pl.when(shard < ctx)
        def _():
            z_copy(shard, ctx).wait_recv()
            for step in range(1, n_head):
                x_copy(shard, head, step).start()
            for step in range(1, n_sub):
                s_copy(shard, head, sub, step).start()

    for shard in range(n - 2, -1, -1):

        @pl.when(shard < ctx)
        def _():
            for step in range(1, n_head):
                x = lax.rem(head + step, n_head)
                x_copy(shard, x, step).wait_recv()
                for s_step in range(1, n_sub):
                    s_copy(shard, x, sub, s_step).start()

    for shard in range(n - 2, -1, -1):

        @pl.when(shard < ctx)
        def _():
            for x in range(n_head):
                for s_step in range(1, n_sub):
                    s_copy(shard, x, lax.rem(sub + s_step, n_sub), s_step).wait_recv()

    length = length_ref[0]
    row_pos = ctx * rows + lax.broadcasted_iota(jnp.int32, (rows, 1), 0)
    last_key = jnp.minimum(row_pos, length - 1)
    live = row_pos < length
    n_chunks = n * rows // chunk

    def expand(pair, chunk_index):
        at = pl.multiple_of(chunk_index * chunk, chunk)
        block = pl.ds(at, chunk)
        expanded = jnp.dot(
            keys[block, pl.ds(0, width)], w_buf[pair], preferred_element_type=jnp.float32
        ).astype(jnp.bfloat16)
        allowed = at + lax.broadcasted_iota(jnp.int32, (rows, chunk), 1) <= last_key
        return expanded, keys[block, pl.ds(width, 2 * ROPE)], allowed

    def head_scores(pair, which, expanded, key_rope, allowed):
        k = jnp.concatenate([expanded[:, which * KVDIM : which * KVDIM + NOPE], key_rope], 1)
        scores = lax.dot_general(
            q_ready[2 * pair + which], k, (((1,), (1,)), ((), ())), preferred_element_type=jnp.float32
        )
        return jnp.where(allowed, scores, -1e30)

    def head_mix(which, weights, expanded):
        values = expanded[:, which * KVDIM + NOPE : (which + 1) * KVDIM]
        v = jnp.concatenate([values, jnp.ones_like(values)], 1)
        return jnp.dot(weights.astype(jnp.bfloat16), v, preferred_element_type=jnp.float32)

    def finish(pair, which, mixed):
        result = jnp.where(live, mixed[:, :VDIM] / mixed[:, VDIM:], 0.0)
        out_buf[pair, :, which * VDIM : (which + 1) * VDIM] = result.astype(jnp.bfloat16)

    def out_copy(pair):
        return pltpu.make_async_copy(
            out_buf.at[pair],
            out.at[:, pl.ds(pl.multiple_of(pair * 2 * VDIM, 2 * VDIM), 2 * VDIM)],
            out_sem.at[pair],
        )

    def attend(pair, carry):
        w_load(pair).wait()
        if n_chunks == 1:
            expanded, key_rope, allowed = expand(pair, 0)
            for which in range(2):
                scores = head_scores(pair, which, expanded, key_rope, allowed)
                top = jnp.max(scores, -1, keepdims=True)
                weights = jnp.exp2((scores - top) * SCORE_SCALE)
                finish(pair, which, head_mix(which, weights, expanded))
        else:

            def one_chunk(chunk_index, state):
                expanded, key_rope, allowed = expand(pair, chunk_index)
                later = []
                for which in range(2):
                    top, mixed = state[which]
                    scores = head_scores(pair, which, expanded, key_rope, allowed)
                    new_top = jnp.maximum(top, jnp.max(scores, -1, keepdims=True))
                    weights = jnp.exp2((scores - new_top) * SCORE_SCALE)
                    fade = jnp.exp2((top - new_top) * SCORE_SCALE)
                    later.append((new_top, mixed * fade + head_mix(which, weights, expanded)))
                return tuple(later)

            blank = (jnp.full((rows, 1), -1e30, jnp.float32), jnp.zeros((rows, 2 * VDIM), jnp.float32))
            needed = (ctx * rows) // chunk + 1
            state = lax.fori_loop(0, needed, one_chunk, (blank, blank))
            for which in range(2):
                finish(pair, which, state[which][1])
        out_copy(pair).start()
        return carry

    lax.fori_loop(0, pairs, attend, 0)

    for pair in range(pairs):
        out_copy(pair).wait()
    for target in range(n - 1, 0, -1):

        @pl.when(ctx < target)
        def _():
            z_copy(ctx, target).wait_send()

    for shard in range(n - 2, -1, -1):

        @pl.when(shard < ctx)
        def _():
            for step in range(1, n_head):
                x_copy(shard, head, step).wait_send()
            for step in range(1, n_sub):
                for x in range(n_head):
                    s_copy(shard, x, sub, step).wait_send()


def per_device(n, n_head, n_sub, queries, latent, rope_keys, latent_gain, up_weight, prompt_length):
    rows, width = latent.shape
    pairs = up_weight.shape[1] // (2 * KVDIM)
    heads = 2 * pairs
    tokens = n * rows
    chunk = tokens if tokens <= 512 else (512 if tokens % 512 == 0 else rows)
    anywhere = pl.BlockSpec(memory_space=pl.ANY)
    dma = pltpu.SemaphoreType.DMA
    cost = pl.CostEstimate(
        flops=2 * tokens * width * up_weight.shape[1] + 2 * heads * rows * tokens * (QDIM + VDIM),
        bytes_accessed=2 * (queries.size + up_weight.size + rows * heads * VDIM),
        transcendentals=heads * rows * tokens,
    )
    return pl.pallas_call(
        functools.partial(kernel, n, n_head, n_sub, chunk),
        out_shape=jax.ShapeDtypeStruct((rows, heads * VDIM), jnp.bfloat16),
        in_specs=[pl.BlockSpec(memory_space=pltpu.SMEM)] + [anywhere] * 5,
        out_specs=anywhere,
        scratch_shapes=[
            pltpu.VMEM((tokens, width + 2 * ROPE), jnp.bfloat16),
            pltpu.VMEM(queries.shape, jnp.bfloat16),
            pltpu.VMEM((heads, rows, NOPE + 2 * ROPE), jnp.bfloat16),
            pltpu.VMEM((pairs, width, 2 * KVDIM), jnp.bfloat16),
            pltpu.VMEM((rows, width), jnp.bfloat16),
            pltpu.VMEM((rows, ROPE), jnp.bfloat16),
            pltpu.VMEM((width,), jnp.float32),
            pltpu.VMEM((pairs, rows, 2 * VDIM), jnp.bfloat16),
            dma((4,)),
            dma((pairs,)),
            dma((pairs,)),
            dma((n,)),
            dma((n,)),
            dma((n, n_head)),
            dma((n, n_head)),
            dma((n, n_head, n_sub)),
            dma((n, n_head, n_sub)),
        ],
        compiler_params=pltpu.CompilerParams(
            collective_id=0, has_side_effects=True, vmem_limit_bytes=48 * 1024 * 1024
        ),
        cost_estimate=cost,
        name="mla_prefill",
    )(prompt_length, queries, latent, rope_keys, latent_gain, up_weight)


def solution(mesh):
    placed = (
        P(("parts", "ctx"), ("head", "sub")),
        P(("parts", "ctx"), None),
        P(("parts", "ctx"), None),
        P(),
        P(None, ("head", "sub")),
        P("parts"),
    )
    return jax.shard_map(
        functools.partial(per_device, mesh.shape["ctx"], mesh.shape["head"], mesh.shape["sub"]),
        mesh=mesh,
        in_specs=placed,
        out_specs=P(("parts", "ctx"), ("head", "sub")),
        check_vma=False,
    )
```

time: 47 us -> 30.6 us (0.65)
  the two profiles are of different devices: /device:TPU:0 before, /device:TPU:17 now
where the time goes in v1:
time: 30.6 us; the launch traced here: 30.3 us
  Pallas kernels  23.1 us (75%)
  local copies, waits for them, and re-layouts  6.53 us (21%)
  between operations  0.67 us (2%)
    pallas_call x1, Pallas kernels, per_device(): pl.pallas_call(functools.partial(kernel, n, n_head, n_sub, chunk), out_sh...  23.1 us
    unnamed x10, local copies, waits for them, and re-layouts  6.53 us

profile of v1, /device:TPU:17, one launch (start us, length us, event | category | flops | bytes accessed | tf_op | source)
XLA Modules:
  0.0 30.3 jit_solution(7962172036022336158)
XLA Ops:
  0.7 0.8 %copy.7.rope_keys = bf16[128,64]{1,0:T(8,128)(2,1)S(1)} copy(bf16[128,64]{0,1:T(8,128)(2,1)} %param.8) | data formatting | bytes 32768 | tf_op args[2]
  1.5 0.0 copy-start
  1.5 2.2 %copy-done = bf16[512,4096]{1,0:T(8,128)(2,1)S(1)} copy-done((bf16[512,4096]{1,0:T(8,128)(2,1)S(1)}, bf16[512,4096]{1,0:T(8,128)(2,1)}, u32[]{:S(2)}) %copy-start) | copy-done | bytes 4194328
  3.7 0.0 copy-start.1
  3.7 1.1 %copy-done.1 = bf16[128,3072]{1,0:T(8,128)(2,1)S(1)} copy-done((bf16[128,3072]{1,0:T(8,128)(2,1)S(1)}, bf16[128,3072]{1,0:T(8,128)(2,1)}, u32[]{:S(2)}) %copy-start.1) | copy-done | bytes 786456
  4.8 0.0 copy-start.2
  4.8 0.9 %copy-done.2 = bf16[128,512]{1,0:T(8,128)(2,1)S(1)} copy-done((bf16[128,512]{1,0:T(8,128)(2,1)S(1)}, bf16[128,512]{1,0:T(8,128)(2,1)}, u32[]{:S(2)}) %copy-start.2) | copy-done | bytes 131096
  5.7 0.0 copy-start.3
  5.7 0.7 %copy-done.3 = f32[512]{0:T(512)S(1)} copy-done((f32[512]{0:T(512)S(1)}, f32[512]{0:T(512)}, u32[]{:S(2)}) %copy-start.3) | copy-done | bytes 2072
  6.4 23.1 %mla_prefill.1 = bf16[128,2048]{1,0:T(8,128)(2,1)S(1)} custom-call(s32[1]{0:T(128)S(6)} %copy.9.length_ref, bf16[128,3072]{1,0:T(8,128)(2,1)S(1)} %copy-done.1, bf16[128,512]{1,0:T(8,128)(2,1)S(1)} %copy-done.2, bf16[128,64]{1,0:T(8,128)(2,1)S(1)} %copy.7.rope_keys, f32[512]{0:T(512)S(1)} %copy-done.3, bf16[512,4096]{1,0:T(8,128)(2,1)S(1)} %copy-done), custom_call_target="tpu_custom_call" | custom-call | flops 2818572288 | bytes 5505024 | tf_op jit(solution)/shard_map/mla_prefill/pallas_call | solution.py:308
  29.5 0.8 %copy.10 = bf16[128,2048]{1,0:T(8,128)(2,1)} copy(bf16[128,2048]{1,0:T(8,128)(2,1)S(1)} %mla_prefill.1) | data formatting | bytes 1048576
Async XLA Ops:
  1.5 2.2 %copy-start = (bf16[512,4096]{1,0:T(8,128)(2,1)S(1)}, bf16[512,4096]{1,0:T(8,128)(2,1)}, u32[]{:S(2)}) copy-start(bf16[512,4096]{1,0:T(8,128)(2,1)} %up_weight.1) | copy-start | bytes 12582916
  3.7 1.1 %copy-start.1 = (bf16[128,3072]{1,0:T(8,128)(2,1)S(1)}, bf16[128,3072]{1,0:T(8,128)(2,1)}, u32[]{:S(2)}) copy-start(bf16[128,3072]{1,0:T(8,128)(2,1)} %queries.1) | copy-start | bytes 2359300
  4.8 0.9 %copy-start.2 = (bf16[128,512]{1,0:T(8,128)(2,1)S(1)}, bf16[128,512]{1,0:T(8,128)(2,1)}, u32[]{:S(2)}) copy-start(bf16[128,512]{1,0:T(8,128)(2,1)} %latent.1) | copy-start | bytes 393220
  5.7 0.7 %copy-start.3 = (f32[512]{0:T(512)S(1)}, f32[512]{0:T(512)}, u32[]{:S(2)}) copy-start(f32[512]{0:T(512)} %latent_gain.1) | copy-start | bytes 6148

commit v2 on v1

--- a/solution.py
+++ b/solution.py
@@ -52,7 +52,7 @@
 def kernel(
     n, n_head, n_sub, chunk,
     length_ref, queries, latent, rope_keys, latent_gain, up_weight, out,
-    keys, q_raw, q_ready, w_buf, lat_buf, rope_buf, gain_buf, out_buf,
+    keys, q_raw, q_ready, w_buf, kv_own, kv_even, kv_odd, lat_buf, rope_buf, gain_buf, out_buf,
     load_sem, w_sem, out_sem, z_send, z_recv, x_send, x_recv, s_send, s_recv,
 ):
     ctx = lax.axis_index("ctx")
@@ -64,6 +64,8 @@
     pair_w = 2 * KVDIM
     pair_q = 2 * QDIM
     piece = rows // (n_head * n_sub)
+    others = (n - 1) * rows
+    n_chunks = n * rows // chunk
 
     loads = [
         pltpu.make_async_copy(latent, lat_buf, load_sem.at[0]),
@@ -111,21 +113,22 @@
     mean = jnp.mean(widened * widened, -1, keepdims=True)
     normed = (widened * lax.rsqrt(mean + 1e-06) * gain_buf[...].reshape(1, width)).astype(jnp.bfloat16)
     rope = rope_buf[...].astype(jnp.float32)
-    rotated = rotate_pair(jnp.concatenate([rope, rope], 1), cosine, sine).astype(jnp.bfloat16)
-    own = pl.ds(pl.multiple_of(ctx * rows, rows), rows)
+    rope = jnp.concatenate([rope, rope], 0).T
+    rotated = rotate_pair(rope, cosine, sine).astype(jnp.bfloat16)
+    own = pl.ds(others, rows)
     keys[own, pl.ds(0, width)] = normed
     keys[own, pl.ds(width, 2 * ROPE)] = rotated
 
     waits = jnp.where(ctx > 0, n_head - 1 + n_sub - 1, 0) + (n - 1 - ctx)
     pl.semaphore_wait(barrier, waits)
 
-    def rows_of(shard, x, s):
-        return pl.ds(pl.multiple_of(shard * rows + (x * n_sub + s) * piece, piece), piece)
+    def rows_of(slot, x, s):
+        return pl.ds(pl.multiple_of(slot * rows + (x * n_sub + s) * piece, piece), piece)
 
     def z_copy(shard, target):
-        where = keys.at[rows_of(shard, head, sub)]
         return pltpu.make_async_remote_copy(
-            where, where, z_send.at[target], z_recv.at[shard],
+            keys.at[rows_of(n - 1, head, sub)], keys.at[rows_of(shard, head, sub)],
+            z_send.at[target], z_recv.at[shard],
             device_id={"ctx": target}, device_id_type=MESH,
         )
 
@@ -149,11 +152,11 @@
         def _():
             z_copy(ctx, target).start()
 
-    for shard in range(1, n):
-
-        @pl.when(ctx < shard)
-        def _():
-            keys[pl.ds(shard * rows, rows), :] = jnp.zeros((rows, width + 2 * ROPE), jnp.bfloat16)
+    for slot in range(n - 1):
+
+        @pl.when(ctx <= slot)
+        def _():
+            keys[pl.ds(slot * rows, rows), :] = jnp.zeros((rows, width + 2 * ROPE), jnp.bfloat16)
 
     loads[3].wait()
     lane = lax.broadcasted_iota(jnp.int32, (rows, 2 * ROPE), 1)
@@ -174,6 +177,19 @@
 
     lax.fori_loop(0, pairs, ready, 0)
 
+    def project(block, pair):
+        return jnp.dot(
+            keys[block, pl.ds(0, width)], w_buf[pair], preferred_element_type=jnp.float32
+        ).astype(jnp.bfloat16)
+
+    def expand_own(pair, carry):
+        w_load(pair).wait()
+        kv_own[pair] = project(own, pair)
+        return carry
+
+    half = pairs // 2
+    lax.fori_loop(0, half, expand_own, 0)
+
     for shard in range(n - 2, -1, -1):
 
         @pl.when(shard < ctx)
@@ -184,6 +200,8 @@
             for step in range(1, n_sub):
                 s_copy(shard, head, sub, step).start()
 
+    lax.fori_loop(half, pairs, expand_own, 0)
+
     for shard in range(n - 2, -1, -1):
 
         @pl.when(shard < ctx)
@@ -206,26 +224,23 @@
     row_pos = ctx * rows + lax.broadcasted_iota(jnp.int32, (rows, 1), 0)
     last_key = jnp.minimum(row_pos, length - 1)
     live = row_pos < length
-    n_chunks = n * rows // chunk
-
-    def expand(pair, chunk_index):
-        at = pl.multiple_of(chunk_index * chunk, chunk)
-        block = pl.ds(at, chunk)
-        expanded = jnp.dot(
-            keys[block, pl.ds(0, width)], w_buf[pair], preferred_element_type=jnp.float32
-        ).astype(jnp.bfloat16)
-        allowed = at + lax.broadcasted_iota(jnp.int32, (rows, chunk), 1) <= last_key
-        return expanded, keys[block, pl.ds(width, 2 * ROPE)], allowed
-
-    def head_scores(pair, which, expanded, key_rope, allowed):
-        k = jnp.concatenate([expanded[:, which * KVDIM : which * KVDIM + NOPE], key_rope], 1)
+
+    def allowed_keys(first):
+        slot_pos = first + lax.broadcasted_iota(jnp.int32, (1, chunk), 1)
+        far = n * rows
+        position = jnp.where(
+            slot_pos >= others, slot_pos - others + ctx * rows, jnp.where(slot_pos < ctx * rows, slot_pos, far)
+        )
+        return position <= last_key
+
+    def head_scores(pair, which, key_nope, key_rope, allowed):
+        k = jnp.concatenate([key_nope, key_rope], 1)
         scores = lax.dot_general(
             q_ready[2 * pair + which], k, (((1,), (1,)), ((), ())), preferred_element_type=jnp.float32
         )
         return jnp.where(allowed, scores, -1e30)
 
-    def head_mix(which, weights, expanded):
-        values = expanded[:, which * KVDIM + NOPE : (which + 1) * KVDIM]
+    def head_mix(weights, values):
         v = jnp.concatenate([values, jnp.ones_like(values)], 1)
         return jnp.dot(weights.astype(jnp.bfloat16), v, preferred_element_type=jnp.float32)
 
@@ -240,38 +255,72 @@
             out_sem.at[pair],
         )
 
-    def attend(pair, carry):
-        w_load(pair).wait()
-        if n_chunks == 1:
-            expanded, key_rope, allowed = expand(pair, 0)
+    if n_chunks == 1:
+        allowed = allowed_keys(0)
+        earlier = pl.ds(0, others)
+
+        def expand(pair, kv):
+            kv[earlier, :] = project(earlier, pair)
+            kv[own, :] = kv_own[pair]
+
+        def attend(pair, kv):
+            scores = [
+                head_scores(
+                    pair, which, kv[:, which * KVDIM : which * KVDIM + NOPE], keys[:, width:], allowed
+                )
+                for which in range(2)
+            ]
             for which in range(2):
-                scores = head_scores(pair, which, expanded, key_rope, allowed)
-                top = jnp.max(scores, -1, keepdims=True)
-                weights = jnp.exp2((scores - top) * SCORE_SCALE)
-                finish(pair, which, head_mix(which, weights, expanded))
-        else:
-
-            def one_chunk(chunk_index, state):
-                expanded, key_rope, allowed = expand(pair, chunk_index)
+                top = jnp.max(scores[which], -1, keepdims=True)
+                weights = jnp.exp2((scores[which] - top) * SCORE_SCALE)
+                mixed = head_mix(weights, kv[:, which * KVDIM + NOPE : (which + 1) * KVDIM])
+                finish(pair, which, mixed)
+            out_copy(pair).start()
+
+        expand(0, kv_even)
+
+        def two_pairs(step, carry):
+            expand(2 * step + 1, kv_odd)
+            attend(2 * step, kv_even)
+            expand(lax.rem(2 * step + 2, pairs), kv_even)
+            attend(2 * step + 1, kv_odd)
+            return carry
+
+        lax.fori_loop(0, pairs // 2, two_pairs, 0)
+    else:
+
+        def attend(pair, carry):
+            needed = jnp.minimum((ctx * rows + chunk - 1) // chunk, n_chunks - 1)
+
+            def one_chunk(step, state):
+                index = jnp.where(step == needed, n_chunks - 1, step)
+                at = pl.multiple_of(index * chunk, chunk)
+                block = pl.ds(at, chunk)
+                expanded = project(block, pair)
+                allowed = allowed_keys(at)
                 later = []
                 for which in range(2):
                     top, mixed = state[which]
-                    scores = head_scores(pair, which, expanded, key_rope, allowed)
+                    first = which * KVDIM
+                    scores = head_scores(
+                        pair, which, expanded[:, first : first + NOPE],
+                        keys[block, pl.ds(width, 2 * ROPE)], allowed,
+                    )
                     new_top = jnp.maximum(top, jnp.max(scores, -1, keepdims=True))
-                    weights = jnp.exp2((scores - new_top) * SCORE_SCALE)
+                    weights = jnp.where(allowed, jnp.exp2((scores - new_top) * SCORE_SCALE), 0.0)
                     fade = jnp.exp2((top - new_top) * SCORE_SCALE)
-                    later.append((new_top, mixed * fade + head_mix(which, weights, expanded)))
+                    mix = head_mix(weights, expanded[:, first + NOPE : first + KVDIM])
+                    later.append((new_top, mixed * fade + mix))
                 return tuple(later)
 
             blank = (jnp.full((rows, 1), -1e30, jnp.float32), jnp.zeros((rows, 2 * VDIM), jnp.float32))
-            needed = (ctx * rows) // chunk + 1
-            state = lax.fori_loop(0, needed, one_chunk, (blank, blank))
+            state = lax.fori_loop(0, needed + 1, one_chunk, (blank, blank))
             for which in range(2):
                 finish(pair, which, state[which][1])
-        out_copy(pair).start()
-        return carry
-
-    lax.fori_loop(0, pairs, attend, 0)
+            out_copy(pair).start()
+            return carry
+
+        lax.fori_loop(0, pairs, attend, 0)
 
     for pair in range(pairs):
         out_copy(pair).wait()
@@ -315,8 +364,11 @@
             pltpu.VMEM(queries.shape, jnp.bfloat16),
             pltpu.VMEM((heads, rows, NOPE + 2 * ROPE), jnp.bfloat16),
             pltpu.VMEM((pairs, width, 2 * KVDIM), jnp.bfloat16),
+            pltpu.VMEM((pairs, rows, 2 * KVDIM), jnp.bfloat16),
+            pltpu.VMEM((chunk, 2 * KVDIM), jnp.bfloat16),
+            pltpu.VMEM((chunk, 2 * KVDIM), jnp.bfloat16),
             pltpu.VMEM((rows, width), jnp.bfloat16),
-            pltpu.VMEM((rows, ROPE), jnp.bfloat16),
+            pltpu.VMEM((ROPE, rows), jnp.bfloat16),
             pltpu.VMEM((width,), jnp.float32),
             pltpu.VMEM((pairs, rows, 2 * VDIM), jnp.bfloat16),
             dma((4,)),
@@ -330,11 +382,11 @@
             dma((n, n_head, n_sub)),
         ],
         compiler_params=pltpu.CompilerParams(
-            collective_id=0, has_side_effects=True, vmem_limit_bytes=48 * 1024 * 1024
+            collective_id=0, has_side_effects=True, vmem_limit_bytes=63 * 1024 * 1024
         ),
         cost_estimate=cost,
         name="mla_prefill",
-    )(prompt_length, queries, latent, rope_keys, latent_gain, up_weight)
+    )(prompt_length, queries, latent, rope_keys.T, latent_gain, up_weight)
 
 
 def solution(mesh):

time: 30.6 us -> 22.2 us (0.73)
  local copies, waits for them, and re-layouts: 6.53 us -> 1.88 us
  Pallas kernels: 23.1 us -> 19.5 us
    unnamed x10 -> x1, local copies, waits for them, and re-layouts: 6.53 us -> 1.88 us
    pallas_call x1, Pallas kernels: 23.1 us -> 19.5 us  [per_device(): pl.pallas_call(functools.partial(kernel, n, n_head, n_sub, chunk), out_sh...]
where the time goes in v2:
time: 22.2 us; the launch traced here: 22 us
  Pallas kernels  19.5 us (88%)
  local copies, waits for them, and re-layouts  1.88 us (8%)
  between operations  0.66 us (3%)
    pallas_call x1, Pallas kernels, per_device(): pl.pallas_call(functools.partial(kernel, n, n_head, n_sub, chunk), out_sh...  19.5 us
    unnamed x1, local copies, waits for them, and re-layouts  1.88 us

profile of v2, /device:TPU:17, one launch (start us, length us, event | category | flops | bytes accessed | tf_op | source)
XLA Modules:
  0.0 22.0 jit_solution(11774408468474957405)
XLA Ops:
  0.7 19.5 %mla_prefill.1 = bf16[128,2048]{1,0:T(8,128)(2,1)} custom-call(s32[1]{0:T(128)S(6)} %copy.8.length_ref, bf16[128,3072]{1,0:T(8,128)(2,1)} %queries.1, bf16[128,512]{1,0:T(8,128)(2,1)} %latent.1, bf16[64,128]{1,0:T(8,128)(2,1)} %bitcast.1, f32[512]{0:T(512)} %latent_gain.1, bf16[512,4096]{1,0:T(8,128)(2,1)} %up_weight.1), custom_call_target="tpu_custom_call" | custom-call | flops 2818572288 | bytes 5505024 | tf_op jit(solution)/shard_map/mla_prefill/pallas_call | solution.py:357
  20.1 1.9 %copy.9 = bf16[128,2048]{1,0:T(8,128)(2,1)} copy(bf16[128,2048]{1,0:T(8,128)(2,1)} %mla_prefill.1) | data formatting | bytes 1048576

commit v3 on v2

--- a/solution.py
+++ b/solution.py
@@ -52,8 +52,8 @@
 def kernel(
     n, n_head, n_sub, chunk,
     length_ref, queries, latent, rope_keys, latent_gain, up_weight, out,
-    keys, q_raw, q_ready, w_buf, kv_own, kv_even, kv_odd, lat_buf, rope_buf, gain_buf, out_buf,
-    load_sem, w_sem, out_sem, z_send, z_recv, x_send, x_recv, s_send, s_recv,
+    keys, q_raw, q_ready, w_buf, kv, lat_buf, rope_buf, gain_buf,
+    load_sem, w_sem, z_send, z_recv, x_send, x_recv, s_send, s_recv,
 ):
     ctx = lax.axis_index("ctx")
     head = lax.axis_index("head")
@@ -119,44 +119,13 @@
     keys[own, pl.ds(0, width)] = normed
     keys[own, pl.ds(width, 2 * ROPE)] = rotated
 
-    waits = jnp.where(ctx > 0, n_head - 1 + n_sub - 1, 0) + (n - 1 - ctx)
-    pl.semaphore_wait(barrier, waits)
-
-    def rows_of(slot, x, s):
-        return pl.ds(pl.multiple_of(slot * rows + (x * n_sub + s) * piece, piece), piece)
-
-    def z_copy(shard, target):
-        return pltpu.make_async_remote_copy(
-            keys.at[rows_of(n - 1, head, sub)], keys.at[rows_of(shard, head, sub)],
-            z_send.at[target], z_recv.at[shard],
-            device_id={"ctx": target}, device_id_type=MESH,
-        )
-
-    def x_copy(shard, x, step):
-        where = keys.at[rows_of(shard, x, sub)]
-        return pltpu.make_async_remote_copy(
-            where, where, x_send.at[shard, step], x_recv.at[shard, x],
-            device_id={"head": lax.rem(head + step, n_head)}, device_id_type=MESH,
-        )
-
-    def s_copy(shard, x, s, step):
-        where = keys.at[rows_of(shard, x, s)]
-        return pltpu.make_async_remote_copy(
-            where, where, s_send.at[shard, x, step], s_recv.at[shard, x, s],
-            device_id={"sub": lax.rem(sub + step, n_sub)}, device_id_type=MESH,
-        )
-
-    for target in range(n - 1, 0, -1):
-
-        @pl.when(ctx < target)
-        def _():
-            z_copy(ctx, target).start()
-
     for slot in range(n - 1):
 
         @pl.when(ctx <= slot)
         def _():
             keys[pl.ds(slot * rows, rows), :] = jnp.zeros((rows, width + 2 * ROPE), jnp.bfloat16)
+            if n_chunks == 1:
+                kv[:, pl.ds(slot * rows, rows), :] = jnp.zeros((pairs, rows, pair_w), jnp.bfloat16)
 
     loads[3].wait()
     lane = lax.broadcasted_iota(jnp.int32, (rows, 2 * ROPE), 1)
@@ -177,21 +146,56 @@
 
     lax.fori_loop(0, pairs, ready, 0)
 
+    waits = jnp.where(ctx > 0, n_head - 1 + n_sub - 1, 0) + (n - 1 - ctx)
+    pl.semaphore_wait(barrier, waits)
+
+    def rows_of(slot, x, s):
+        return pl.ds(pl.multiple_of(slot * rows + (x * n_sub + s) * piece, piece), piece)
+
+    def z_copy(shard, target):
+        return pltpu.make_async_remote_copy(
+            keys.at[rows_of(n - 1, head, sub)], keys.at[rows_of(shard, head, sub)],
+            z_send.at[target], z_recv.at[shard],
+            device_id={"ctx": target}, device_id_type=MESH,
+        )
+
+    def x_copy(shard, x, step):
+        where = keys.at[rows_of(shard, x, sub)]
+        return pltpu.make_async_remote_copy(
+            where, where, x_send.at[shard, step], x_recv.at[shard, x],
+            device_id={"head": lax.rem(head + step, n_head)}, device_id_type=MESH,
+        )
+
+    def s_copy(shard, x, s, step):
+        where = keys.at[rows_of(shard, x, s)]
+        return pltpu.make_async_remote_copy(
+            where, where, s_send.at[shard, x, step], s_recv.at[shard, x, s],
+            device_id={"sub": lax.rem(sub + step, n_sub)}, device_id_type=MESH,
+        )
+
+    for target in range(n - 1, 0, -1):
+
+        @pl.when(ctx < target)
+        def _():
+            z_copy(ctx, target).start()
+
     def project(block, pair):
         return jnp.dot(
             keys[block, pl.ds(0, width)], w_buf[pair], preferred_element_type=jnp.float32
         ).astype(jnp.bfloat16)
 
-    def expand_own(pair, carry):
-        w_load(pair).wait()
-        kv_own[pair] = project(own, pair)
-        return carry
-
-    half = pairs // 2
-    lax.fori_loop(0, half, expand_own, 0)
-
-    for shard in range(n - 2, -1, -1):
-
+    def expand(slot, first, last, fresh=False):
+        block = pl.ds(slot * rows, rows)
+
+        def one(pair, carry):
+            if fresh:
+                w_load(pair).wait()
+            kv[pair, block, :] = project(block, pair)
+            return carry
+
+        lax.fori_loop(first, last, one, 0, unroll=2)
+
+    def pass_on(shard):
         @pl.when(shard < ctx)
         def _():
             z_copy(shard, ctx).wait_recv()
@@ -200,10 +204,7 @@
             for step in range(1, n_sub):
                 s_copy(shard, head, sub, step).start()
 
-    lax.fori_loop(half, pairs, expand_own, 0)
-
-    for shard in range(n - 2, -1, -1):
-
+    def pass_to_sibling(shard):
         @pl.when(shard < ctx)
         def _():
             for step in range(1, n_head):
@@ -212,13 +213,58 @@
                 for s_step in range(1, n_sub):
                     s_copy(shard, x, sub, s_step).start()
 
-    for shard in range(n - 2, -1, -1):
-
-        @pl.when(shard < ctx)
-        def _():
-            for x in range(n_head):
-                for s_step in range(1, n_sub):
-                    s_copy(shard, x, lax.rem(sub + s_step, n_sub), s_step).wait_recv()
+    def complete(shard):
+        for x in range(n_head):
+            for s_step in range(1, n_sub):
+                s_copy(shard, x, lax.rem(sub + s_step, n_sub), s_step).wait_recv()
+
+    order = list(range(n - 2, -1, -1))
+    if n_chunks == 1:
+        half = pairs // 2
+        expand(n - 1, 0, half, fresh=True)
+        pass_on(order[0])
+        expand(n - 1, half, pairs, fresh=True)
+        for earlier, later in zip(order[:-1], order[1:]):
+            pass_on(later)
+            pass_to_sibling(earlier)
+        for place, shard in enumerate(order):
+            if place == 0:
+
+                @pl.when(shard < ctx)
+                def _():
+                    if len(order) > 1:
+                        complete(shard)
+                        expand(shard, 0, half)
+
+                pass_to_sibling(order[-1])
+
+                @pl.when(shard < ctx)
+                def _():
+                    if len(order) > 1:
+                        expand(shard, half, pairs)
+                    else:
+                        complete(shard)
+                        expand(shard, 0, pairs)
+
+            else:
+
+                @pl.when(shard < ctx)
+                def _():
+                    complete(shard)
+                    expand(shard, 0, pairs)
+
+    else:
+        for pair in range(pairs):
+            w_load(pair).wait()
+        for shard in order:
+            pass_on(shard)
+        for shard in order:
+            pass_to_sibling(shard)
+        for shard in order:
+
+            @pl.when(shard < ctx)
+            def _():
+                complete(shard)
 
     length = length_ref[0]
     row_pos = ctx * rows + lax.broadcasted_iota(jnp.int32, (rows, 1), 0)
@@ -246,47 +292,27 @@
 
     def finish(pair, which, mixed):
         result = jnp.where(live, mixed[:, :VDIM] / mixed[:, VDIM:], 0.0)
-        out_buf[pair, :, which * VDIM : (which + 1) * VDIM] = result.astype(jnp.bfloat16)
-
-    def out_copy(pair):
-        return pltpu.make_async_copy(
-            out_buf.at[pair],
-            out.at[:, pl.ds(pl.multiple_of(pair * 2 * VDIM, 2 * VDIM), 2 * VDIM)],
-            out_sem.at[pair],
-        )
+        at = pl.multiple_of((2 * pair + which) * VDIM, VDIM)
+        out[:, pl.ds(at, VDIM)] = result.astype(jnp.bfloat16)
 
     if n_chunks == 1:
         allowed = allowed_keys(0)
-        earlier = pl.ds(0, others)
-
-        def expand(pair, kv):
-            kv[earlier, :] = project(earlier, pair)
-            kv[own, :] = kv_own[pair]
-
-        def attend(pair, kv):
+
+        def attend(pair, carry):
             scores = [
                 head_scores(
-                    pair, which, kv[:, which * KVDIM : which * KVDIM + NOPE], keys[:, width:], allowed
+                    pair, which, kv[pair, :, which * KVDIM : which * KVDIM + NOPE], keys[:, width:], allowed
                 )
                 for which in range(2)
             ]
             for which in range(2):
                 top = jnp.max(scores[which], -1, keepdims=True)
                 weights = jnp.exp2((scores[which] - top) * SCORE_SCALE)
-                mixed = head_mix(weights, kv[:, which * KVDIM + NOPE : (which + 1) * KVDIM])
+                mixed = head_mix(weights, kv[pair, :, which * KVDIM + NOPE : (which + 1) * KVDIM])
                 finish(pair, which, mixed)
-            out_copy(pair).start()
-
-        expand(0, kv_even)
-
-        def two_pairs(step, carry):
-            expand(2 * step + 1, kv_odd)
-            attend(2 * step, kv_even)
-            expand(lax.rem(2 * step + 2, pairs), kv_even)
-            attend(2 * step + 1, kv_odd)
             return carry
 
-        lax.fori_loop(0, pairs // 2, two_pairs, 0)
+        lax.fori_loop(0, pairs, attend, 0, unroll=2)
     else:
 
         def attend(pair, carry):
@@ -317,13 +343,10 @@
             state = lax.fori_loop(0, needed + 1, one_chunk, (blank, blank))
             for which in range(2):
                 finish(pair, which, state[which][1])
-            out_copy(pair).start()
             return carry
 
         lax.fori_loop(0, pairs, attend, 0)
 
-    for pair in range(pairs):
-        out_copy(pair).wait()
     for target in range(n - 1, 0, -1):
 
         @pl.when(ctx < target)
@@ -356,23 +379,19 @@
     )
     return pl.pallas_call(
         functools.partial(kernel, n, n_head, n_sub, chunk),
-        out_shape=jax.ShapeDtypeStruct((rows, heads * VDIM), jnp.bfloat16),
+        out_shape=pltpu.VMEM((rows, heads * VDIM), jnp.bfloat16),
         in_specs=[pl.BlockSpec(memory_space=pltpu.SMEM)] + [anywhere] * 5,
-        out_specs=anywhere,
+        out_specs=pl.BlockSpec(memory_space=pltpu.VMEM),
         scratch_shapes=[
             pltpu.VMEM((tokens, width + 2 * ROPE), jnp.bfloat16),
             pltpu.VMEM(queries.shape, jnp.bfloat16),
             pltpu.VMEM((heads, rows, NOPE + 2 * ROPE), jnp.bfloat16),
             pltpu.VMEM((pairs, width, 2 * KVDIM), jnp.bfloat16),
-            pltpu.VMEM((pairs, rows, 2 * KVDIM), jnp.bfloat16),
-            pltpu.VMEM((chunk, 2 * KVDIM), jnp.bfloat16),
-            pltpu.VMEM((chunk, 2 * KVDIM), jnp.bfloat16),
+            pltpu.VMEM((pairs if chunk == tokens else 1, chunk, 2 * KVDIM), jnp.bfloat16),
             pltpu.VMEM((rows, width), jnp.bfloat16),
             pltpu.VMEM((ROPE, rows), jnp.bfloat16),
             pltpu.VMEM((width,), jnp.float32),
-            pltpu.VMEM((pairs, rows, 2 * VDIM), jnp.bfloat16),
             dma((4,)),
-            dma((pairs,)),
             dma((pairs,)),
             dma((n,)),
             dma((n,)),

time: 22.2 us -> 22.3 us (level)
  the two profiles are of different devices: /device:TPU:17 before, /device:TPU:30 now
where the time goes in v3:
time: 22.3 us; the launch traced here: 22.2 us
  Pallas kernels  20.7 us (93%)
  local copies, waits for them, and re-layouts  0.8 us (4%)
  between operations  0.66 us (3%)
    pallas_call x1, Pallas kernels, per_device(): pl.pallas_call(functools.partial(kernel, n, n_head, n_sub, chunk), out_sh...  20.7 us
    unnamed x1, local copies, waits for them, and re-layouts  0.8 us

profile of v3, /device:TPU:30, one launch (start us, length us, event | category | flops | bytes accessed | tf_op | source)
XLA Modules:
  0.0 22.2 jit_solution(528023692511476819)
XLA Ops:
  0.7 20.7 %mla_prefill.1 = bf16[128,2048]{1,0:T(8,128)(2,1)S(1)} custom-call(s32[1]{0:T(128)S(6)} %copy.9.length_ref, bf16[128,3072]{1,0:T(8,128)(2,1)} %queries.1, bf16[128,512]{1,0:T(8,128)(2,1)} %latent.1, bf16[64,128]{1,0:T(8,128)(2,1)} %bitcast.1, f32[512]{0:T(512)} %latent_gain.1, bf16[512,4096]{1,0:T(8,128)(2,1)} %up_weight.1), custom_call_target="tpu_custom_call" | custom-call | flops 2818572288 | bytes 5505024 | tf_op jit(solution)/shard_map/mla_prefill/pallas_call | solution.py:380
  21.4 0.8 %copy.8 = bf16[128,2048]{1,0:T(8,128)(2,1)} copy(bf16[128,2048]{1,0:T(8,128)(2,1)S(1)} %mla_prefill.1) | data formatting | bytes 1048576

commit v4 on v3

--- a/solution.py
+++ b/solution.py
@@ -13,6 +13,7 @@
 VDIM = 128
 QDIM = NOPE + ROPE
 KVDIM = NOPE + VDIM
+ONES = 16
 MESH = pl.DeviceIdType.MESH
 SCORE_SCALE = math.log2(math.e) / math.sqrt(NOPE + ROPE)
 
@@ -52,7 +53,7 @@
 def kernel(
     n, n_head, n_sub, chunk,
     length_ref, queries, latent, rope_keys, latent_gain, up_weight, out,
-    keys, q_raw, q_ready, w_buf, kv, lat_buf, rope_buf, gain_buf,
+    keys, q_raw, q_ready, w_buf, value_w, values_t, lat_buf, rope_buf, gain_buf,
     load_sem, w_sem, z_send, z_recv, x_send, x_recv, s_send, s_recv,
 ):
     ctx = lax.axis_index("ctx")
@@ -124,8 +125,6 @@
         @pl.when(ctx <= slot)
         def _():
             keys[pl.ds(slot * rows, rows), :] = jnp.zeros((rows, width + 2 * ROPE), jnp.bfloat16)
-            if n_chunks == 1:
-                kv[:, pl.ds(slot * rows, rows), :] = jnp.zeros((pairs, rows, pair_w), jnp.bfloat16)
 
     loads[3].wait()
     lane = lax.broadcasted_iota(jnp.int32, (rows, 2 * ROPE), 1)
@@ -184,17 +183,6 @@
             keys[block, pl.ds(0, width)], w_buf[pair], preferred_element_type=jnp.float32
         ).astype(jnp.bfloat16)
 
-    def expand(slot, first, last, fresh=False):
-        block = pl.ds(slot * rows, rows)
-
-        def one(pair, carry):
-            if fresh:
-                w_load(pair).wait()
-            kv[pair, block, :] = project(block, pair)
-            return carry
-
-        lax.fori_loop(first, last, one, 0, unroll=2)
-
     def pass_on(shard):
         @pl.when(shard < ctx)
         def _():
@@ -220,51 +208,33 @@
 
     order = list(range(n - 2, -1, -1))
     if n_chunks == 1:
+
+        def turn(pair, carry):
+            w_load(pair).wait()
+            for which in range(2):
+                first = which * KVDIM + NOPE
+                at = pl.multiple_of((2 * pair + which) * VDIM, VDIM)
+                value_w[pl.ds(at, VDIM), :] = w_buf[pair, :, first : first + VDIM].T
+            return carry
+
         half = pairs // 2
-        expand(n - 1, 0, half, fresh=True)
+        values_t[:, pl.ds(VDIM, ONES), :] = jnp.ones((2 * pairs, ONES, chunk), jnp.bfloat16)
+        lax.fori_loop(0, half, turn, 0)
         pass_on(order[0])
-        expand(n - 1, half, pairs, fresh=True)
-        for earlier, later in zip(order[:-1], order[1:]):
-            pass_on(later)
-            pass_to_sibling(earlier)
-        for place, shard in enumerate(order):
-            if place == 0:
-
-                @pl.when(shard < ctx)
-                def _():
-                    if len(order) > 1:
-                        complete(shard)
-                        expand(shard, 0, half)
-
-                pass_to_sibling(order[-1])
-
-                @pl.when(shard < ctx)
-                def _():
-                    if len(order) > 1:
-                        expand(shard, half, pairs)
-                    else:
-                        complete(shard)
-                        expand(shard, 0, pairs)
-
-            else:
-
-                @pl.when(shard < ctx)
-                def _():
-                    complete(shard)
-                    expand(shard, 0, pairs)
-
+        lax.fori_loop(half, pairs, turn, 0)
     else:
         for pair in range(pairs):
             w_load(pair).wait()
-        for shard in order:
-            pass_on(shard)
-        for shard in order:
-            pass_to_sibling(shard)
-        for shard in order:
-
-            @pl.when(shard < ctx)
-            def _():
-                complete(shard)
+        pass_on(order[0])
+    for earlier, later in zip(order[:-1], order[1:]):
+        pass_on(later)
+        pass_to_sibling(earlier)
+    pass_to_sibling(order[-1])
+    for shard in order:
+
+        @pl.when(shard < ctx)
+        def _():
+            complete(shard)
 
     length = length_ref[0]
     row_pos = ctx * rows + lax.broadcasted_iota(jnp.int32, (rows, 1), 0)
@@ -296,20 +266,46 @@
         out[:, pl.ds(at, VDIM)] = result.astype(jnp.bfloat16)
 
     if n_chunks == 1:
-        allowed = allowed_keys(0)
+        group = pairs
+        column = lax.broadcasted_iota(jnp.int32, (1, rows), 1) + ctx * rows
+        slot_pos = lax.broadcasted_iota(jnp.int32, (chunk, 1), 0)
+        key_pos = jnp.where(
+            slot_pos >= others, slot_pos - others + ctx * rows,
+            jnp.where(slot_pos < ctx * rows, slot_pos, n * rows),
+        )
+        allowed = key_pos <= jnp.minimum(column, length - 1)
+        live_t = column < length
+
+        for part in range(2 * pairs // group):
+            spread = lax.dot_general(
+                value_w[pl.ds(part * group * VDIM, group * VDIM), :], keys[:, pl.ds(0, width)],
+                (((1,), (1,)), ((), ())), preferred_element_type=jnp.float32,
+            ).astype(jnp.bfloat16)
+            values_t[pl.ds(part * group, group), pl.ds(0, VDIM), :] = spread.reshape(group, VDIM, chunk)
 
         def attend(pair, carry):
-            scores = [
-                head_scores(
-                    pair, which, kv[pair, :, which * KVDIM : which * KVDIM + NOPE], keys[:, width:], allowed
+            key_w = jnp.concatenate(
+                [w_buf[pair, :, which * KVDIM : which * KVDIM + NOPE] for which in range(2)], 1
+            )
+            key_nope = jnp.dot(
+                keys[:, pl.ds(0, width)], key_w, preferred_element_type=jnp.float32
+            ).astype(jnp.bfloat16)
+            key_rope = keys[:, pl.ds(width, 2 * ROPE)]
+            for which in range(2):
+                k = jnp.concatenate([key_nope[:, which * NOPE : (which + 1) * NOPE], key_rope], 1)
+                scores = lax.dot_general(
+                    k, q_ready[2 * pair + which], (((1,), (1,)), ((), ())),
+                    preferred_element_type=jnp.float32,
                 )
-                for which in range(2)
-            ]
-            for which in range(2):
-                top = jnp.max(scores[which], -1, keepdims=True)
-                weights = jnp.exp2((scores[which] - top) * SCORE_SCALE)
-                mixed = head_mix(weights, kv[pair, :, which * KVDIM + NOPE : (which + 1) * KVDIM])
-                finish(pair, which, mixed)
+                scores = jnp.where(allowed, scores, -1e30)
+                top = jnp.max(scores, 0, keepdims=True)
+                weights = jnp.exp2((scores - top) * SCORE_SCALE).astype(jnp.bfloat16)
+                mixed = jnp.dot(
+                    values_t[2 * pair + which], weights, preferred_element_type=jnp.float32
+                )
+                result = jnp.where(live_t, mixed[:VDIM] / mixed[VDIM : VDIM + 1], 0.0)
+                at = pl.multiple_of((2 * pair + which) * VDIM, VDIM)
+                out[:, pl.ds(at, VDIM)] = result.T.astype(jnp.bfloat16)
             return carry
 
         lax.fori_loop(0, pairs, attend, 0, unroll=2)
@@ -387,7 +383,8 @@
             pltpu.VMEM(queries.shape, jnp.bfloat16),
             pltpu.VMEM((heads, rows, NOPE + 2 * ROPE), jnp.bfloat16),
             pltpu.VMEM((pairs, width, 2 * KVDIM), jnp.bfloat16),
-            pltpu.VMEM((pairs if chunk == tokens else 1, chunk, 2 * KVDIM), jnp.bfloat16),
+            pltpu.VMEM((heads * VDIM, width), jnp.bfloat16),
+            pltpu.VMEM((heads, VDIM + ONES, chunk), jnp.bfloat16),
             pltpu.VMEM((rows, width), jnp.bfloat16),
             pltpu.VMEM((ROPE, rows), jnp.bfloat16),
             pltpu.VMEM((width,), jnp.float32),

time: 22.3 us -> 26.8 us (1.20)
  the two profiles are of different devices: /device:TPU:30 before, /device:TPU:31 now
where the time goes in v4:
time: 26.8 us; the launch traced here: 26.6 us
  Pallas kernels  25.2 us (94%)
  local copies, waits for them, and re-layouts  0.8 us (3%)
  between operations  0.66 us (2%)
    pallas_call x1, Pallas kernels, per_device(): pl.pallas_call(functools.partial(kernel, n, n_head, n_sub, chunk), out_sh...  25.2 us
    unnamed x1, local copies, waits for them, and re-layouts  0.8 us

profile of v4, /device:TPU:31, one launch (start us, length us, event | category | flops | bytes accessed | tf_op | source)
XLA Modules:
  0.0 26.6 jit_solution(922142125088988501)
XLA Ops:
  0.7 25.2 %mla_prefill.1 = bf16[128,2048]{1,0:T(8,128)(2,1)S(1)} custom-call(s32[1]{0:T(128)S(6)} %copy.9.length_ref, bf16[128,3072]{1,0:T(8,128)(2,1)} %queries.1, bf16[128,512]{1,0:T(8,128)(2,1)} %latent.1, bf16[64,128]{1,0:T(8,128)(2,1)} %bitcast.1, f32[512]{0:T(512)} %latent_gain.1, bf16[512,4096]{1,0:T(8,128)(2,1)} %up_weight.1), custom_call_target="tpu_custom_call" | custom-call | flops 2818572288 | bytes 5505024 | tf_op jit(solution)/shard_map/mla_prefill/pallas_call | solution.py:376
  25.9 0.8 %copy.8 = bf16[128,2048]{1,0:T(8,128)(2,1)} copy(bf16[128,2048]{1,0:T(8,128)(2,1)S(1)} %mla_prefill.1) | data formatting | bytes 1048576

commit v5 on v3

--- a/solution.py
+++ b/solution.py
@@ -52,7 +52,7 @@
 def kernel(
     n, n_head, n_sub, chunk,
     length_ref, queries, latent, rope_keys, latent_gain, up_weight, out,
-    keys, q_raw, q_ready, w_buf, kv, lat_buf, rope_buf, gain_buf,
+    keys, q_raw, q_ready, w_buf, kv, own_top, own_mix, lat_buf, rope_buf, gain_buf,
     load_sem, w_sem, z_send, z_recv, x_send, x_recv, s_send, s_recv,
 ):
     ctx = lax.axis_index("ctx")
@@ -124,8 +124,6 @@
         @pl.when(ctx <= slot)
         def _():
             keys[pl.ds(slot * rows, rows), :] = jnp.zeros((rows, width + 2 * ROPE), jnp.bfloat16)
-            if n_chunks == 1:
-                kv[:, pl.ds(slot * rows, rows), :] = jnp.zeros((pairs, rows, pair_w), jnp.bfloat16)
 
     loads[3].wait()
     lane = lax.broadcasted_iota(jnp.int32, (rows, 2 * ROPE), 1)
@@ -184,17 +182,6 @@
             keys[block, pl.ds(0, width)], w_buf[pair], preferred_element_type=jnp.float32
         ).astype(jnp.bfloat16)
 
-    def expand(slot, first, last, fresh=False):
-        block = pl.ds(slot * rows, rows)
-
-        def one(pair, carry):
-            if fresh:
-                w_load(pair).wait()
-            kv[pair, block, :] = project(block, pair)
-            return carry
-
-        lax.fori_loop(first, last, one, 0, unroll=2)
-
     def pass_on(shard):
         @pl.when(shard < ctx)
         def _():
@@ -218,61 +205,13 @@
             for s_step in range(1, n_sub):
                 s_copy(shard, x, lax.rem(sub + s_step, n_sub), s_step).wait_recv()
 
-    order = list(range(n - 2, -1, -1))
-    if n_chunks == 1:
-        half = pairs // 2
-        expand(n - 1, 0, half, fresh=True)
-        pass_on(order[0])
-        expand(n - 1, half, pairs, fresh=True)
-        for earlier, later in zip(order[:-1], order[1:]):
-            pass_on(later)
-            pass_to_sibling(earlier)
-        for place, shard in enumerate(order):
-            if place == 0:
-
-                @pl.when(shard < ctx)
-                def _():
-                    if len(order) > 1:
-                        complete(shard)
-                        expand(shard, 0, half)
-
-                pass_to_sibling(order[-1])
-
-                @pl.when(shard < ctx)
-                def _():
-                    if len(order) > 1:
-                        expand(shard, half, pairs)
-                    else:
-                        complete(shard)
-                        expand(shard, 0, pairs)
-
-            else:
-
-                @pl.when(shard < ctx)
-                def _():
-                    complete(shard)
-                    expand(shard, 0, pairs)
-
-    else:
-        for pair in range(pairs):
-            w_load(pair).wait()
-        for shard in order:
-            pass_on(shard)
-        for shard in order:
-            pass_to_sibling(shard)
-        for shard in order:
-
-            @pl.when(shard < ctx)
-            def _():
-                complete(shard)
-
     length = length_ref[0]
     row_pos = ctx * rows + lax.broadcasted_iota(jnp.int32, (rows, 1), 0)
     last_key = jnp.minimum(row_pos, length - 1)
     live = row_pos < length
 
-    def allowed_keys(first):
-        slot_pos = first + lax.broadcasted_iota(jnp.int32, (1, chunk), 1)
+    def allowed_keys(first, count):
+        slot_pos = first + lax.broadcasted_iota(jnp.int32, (1, count), 1)
         far = n * rows
         position = jnp.where(
             slot_pos >= others, slot_pos - others + ctx * rows, jnp.where(slot_pos < ctx * rows, slot_pos, far)
@@ -295,21 +234,64 @@
         at = pl.multiple_of((2 * pair + which) * VDIM, VDIM)
         out[:, pl.ds(at, VDIM)] = result.astype(jnp.bfloat16)
 
+    def own_part(pair, carry):
+        w_load(pair).wait()
+        expanded = project(own, pair)
+        allowed = allowed_keys(others, rows)
+        for which in range(2):
+            first = which * KVDIM
+            scores = head_scores(
+                pair, which, expanded[:, first : first + NOPE], keys[own, pl.ds(width, 2 * ROPE)], allowed
+            )
+            top = jnp.max(scores, -1, keepdims=True)
+            weights = jnp.exp2((scores - top) * SCORE_SCALE)
+            own_top[2 * pair + which] = jnp.broadcast_to(top, (rows, VDIM))
+            own_mix[2 * pair + which] = head_mix(weights, expanded[:, first + NOPE : first + KVDIM])
+        return carry
+
+    order = list(range(n - 2, -1, -1))
+    bounds = [pairs * k // n for k in range(n + 1)]
+    for k in range(n):
+        if n_chunks == 1:
+            lax.fori_loop(bounds[k], bounds[k + 1], own_part, 0, unroll=True)
+        else:
+            for pair in range(bounds[k], bounds[k + 1]):
+                w_load(pair).wait()
+        if k < n - 1:
+            pass_on(order[k])
+        if k > 0:
+            pass_to_sibling(order[k - 1])
+    for shard in order:
+
+        @pl.when(shard < ctx)
+        def _():
+            complete(shard)
+
     if n_chunks == 1:
-        allowed = allowed_keys(0)
+        allowed = allowed_keys(0, others)
+        earlier = pl.ds(0, others)
+
+        def expand(pair, carry):
+            kv[pair] = project(earlier, pair)
+            return carry
+
+        lax.fori_loop(0, pairs, expand, 0, unroll=2)
 
         def attend(pair, carry):
             scores = [
                 head_scores(
-                    pair, which, kv[pair, :, which * KVDIM : which * KVDIM + NOPE], keys[:, width:], allowed
+                    pair, which, kv[pair, :, which * KVDIM : which * KVDIM + NOPE],
+                    keys[earlier, pl.ds(width, 2 * ROPE)], allowed,
                 )
                 for which in range(2)
             ]
             for which in range(2):
-                top = jnp.max(scores[which], -1, keepdims=True)
+                before = own_top[2 * pair + which][:, :1]
+                top = jnp.maximum(before, jnp.max(scores[which], -1, keepdims=True))
                 weights = jnp.exp2((scores[which] - top) * SCORE_SCALE)
+                fade = jnp.exp2((before - top) * SCORE_SCALE)
                 mixed = head_mix(weights, kv[pair, :, which * KVDIM + NOPE : (which + 1) * KVDIM])
-                finish(pair, which, mixed)
+                finish(pair, which, mixed + own_mix[2 * pair + which] * fade)
             return carry
 
         lax.fori_loop(0, pairs, attend, 0, unroll=2)
@@ -323,7 +305,7 @@
                 at = pl.multiple_of(index * chunk, chunk)
                 block = pl.ds(at, chunk)
                 expanded = project(block, pair)
-                allowed = allowed_keys(at)
+                allowed = allowed_keys(at, chunk)
                 later = []
                 for which in range(2):
                     top, mixed = state[which]
@@ -387,7 +369,9 @@
             pltpu.VMEM(queries.shape, jnp.bfloat16),
             pltpu.VMEM((heads, rows, NOPE + 2 * ROPE), jnp.bfloat16),
             pltpu.VMEM((pairs, width, 2 * KVDIM), jnp.bfloat16),
-            pltpu.VMEM((pairs if chunk == tokens else 1, chunk, 2 * KVDIM), jnp.bfloat16),
+            pltpu.VMEM((pairs, chunk - rows if chunk == tokens else 16, 2 * KVDIM), jnp.bfloat16),
+            pltpu.VMEM((heads, rows, VDIM), jnp.float32),
+            pltpu.VMEM((heads, rows, 2 * VDIM), jnp.float32),
             pltpu.VMEM((rows, width), jnp.bfloat16),
             pltpu.VMEM((ROPE, rows), jnp.bfloat16),
             pltpu.VMEM((width,), jnp.float32),

time: 22.3 us -> 24.3 us (1.090)
  the two profiles are of different devices: /device:TPU:30 before, /device:TPU:25 now
where the time goes in v5:
time: 24.3 us; the launch traced here: 24.2 us
  Pallas kernels  22.7 us (93%)
  local copies, waits for them, and re-layouts  0.8 us (3%)
  between operations  0.66 us (3%)
    pallas_call x1, Pallas kernels, per_device(): pl.pallas_call(functools.partial(kernel, n, n_head, n_sub, chunk), out_sh...  22.7 us
    unnamed x1, local copies, waits for them, and re-layouts  0.8 us

profile of v5, /device:TPU:25, one launch (start us, length us, event | category | flops | bytes accessed | tf_op | source)
XLA Modules:
  0.0 24.2 jit_solution(11142856178596184231)
XLA Ops:
  0.7 22.7 %mla_prefill.1 = bf16[128,2048]{1,0:T(8,128)(2,1)S(1)} custom-call(s32[1]{0:T(128)S(6)} %copy.9.length_ref, bf16[128,3072]{1,0:T(8,128)(2,1)} %queries.1, bf16[128,512]{1,0:T(8,128)(2,1)} %latent.1, bf16[64,128]{1,0:T(8,128)(2,1)} %bitcast.1, f32[512]{0:T(512)} %latent_gain.1, bf16[512,4096]{1,0:T(8,128)(2,1)} %up_weight.1), custom_call_target="tpu_custom_call" | custom-call | flops 2818572288 | bytes 5505024 | tf_op jit(solution)/shard_map/mla_prefill/pallas_call | solution.py:362
  23.4 0.8 %copy.8 = bf16[128,2048]{1,0:T(8,128)(2,1)} copy(bf16[128,2048]{1,0:T(8,128)(2,1)S(1)} %mla_prefill.1) | data formatting | bytes 1048576

commit v6 on v3

--- a/solution.py
+++ b/solution.py
@@ -124,8 +124,6 @@
         @pl.when(ctx <= slot)
         def _():
             keys[pl.ds(slot * rows, rows), :] = jnp.zeros((rows, width + 2 * ROPE), jnp.bfloat16)
-            if n_chunks == 1:
-                kv[:, pl.ds(slot * rows, rows), :] = jnp.zeros((pairs, rows, pair_w), jnp.bfloat16)
 
     loads[3].wait()
     lane = lax.broadcasted_iota(jnp.int32, (rows, 2 * ROPE), 1)
@@ -184,16 +182,14 @@
             keys[block, pl.ds(0, width)], w_buf[pair], preferred_element_type=jnp.float32
         ).astype(jnp.bfloat16)
 
-    def expand(slot, first, last, fresh=False):
-        block = pl.ds(slot * rows, rows)
-
+    def expand(block, fresh):
         def one(pair, carry):
             if fresh:
                 w_load(pair).wait()
             kv[pair, block, :] = project(block, pair)
             return carry
 
-        lax.fori_loop(first, last, one, 0, unroll=2)
+        lax.fori_loop(0, pairs, one, 0, unroll=2)
 
     def pass_on(shard):
         @pl.when(shard < ctx)
@@ -220,51 +216,20 @@
 
     order = list(range(n - 2, -1, -1))
     if n_chunks == 1:
-        half = pairs // 2
-        expand(n - 1, 0, half, fresh=True)
-        pass_on(order[0])
-        expand(n - 1, half, pairs, fresh=True)
-        for earlier, later in zip(order[:-1], order[1:]):
-            pass_on(later)
-            pass_to_sibling(earlier)
-        for place, shard in enumerate(order):
-            if place == 0:
-
-                @pl.when(shard < ctx)
-                def _():
-                    if len(order) > 1:
-                        complete(shard)
-                        expand(shard, 0, half)
-
-                pass_to_sibling(order[-1])
-
-                @pl.when(shard < ctx)
-                def _():
-                    if len(order) > 1:
-                        expand(shard, half, pairs)
-                    else:
-                        complete(shard)
-                        expand(shard, 0, pairs)
-
-            else:
-
-                @pl.when(shard < ctx)
-                def _():
-                    complete(shard)
-                    expand(shard, 0, pairs)
-
+        expand(own, True)
     else:
         for pair in range(pairs):
             w_load(pair).wait()
-        for shard in order:
-            pass_on(shard)
-        for shard in order:
-            pass_to_sibling(shard)
-        for shard in order:
-
-            @pl.when(shard < ctx)
-            def _():
-                complete(shard)
+    pass_on(order[0])
+    for earlier, later in zip(order[:-1], order[1:]):
+        pass_on(later)
+        pass_to_sibling(earlier)
+    pass_to_sibling(order[-1])
+    for shard in order:
+
+        @pl.when(shard < ctx)
+        def _():
+            complete(shard)
 
     length = length_ref[0]
     row_pos = ctx * rows + lax.broadcasted_iota(jnp.int32, (rows, 1), 0)
@@ -298,21 +263,32 @@
     if n_chunks == 1:
         allowed = allowed_keys(0)
 
-        def attend(pair, carry):
+        expand(pl.ds(0, others), False)
+        together = 4 if pairs % 2 == 0 else 2
+
+        def attend(step, carry):
+            where = [(step * (together // 2) + k // 2, k % 2) for k in range(together)]
+            key_rope = keys[:, pl.ds(width, 2 * ROPE)]
             scores = [
                 head_scores(
-                    pair, which, kv[pair, :, which * KVDIM : which * KVDIM + NOPE], keys[:, width:], allowed
+                    pair, which, kv[pair, :, which * KVDIM : which * KVDIM + NOPE], key_rope, allowed
                 )
-                for which in range(2)
+                for pair, which in where
             ]
-            for which in range(2):
-                top = jnp.max(scores[which], -1, keepdims=True)
-                weights = jnp.exp2((scores[which] - top) * SCORE_SCALE)
-                mixed = head_mix(weights, kv[pair, :, which * KVDIM + NOPE : (which + 1) * KVDIM])
+            tops = [jnp.max(score, -1, keepdims=True) for score in scores]
+            weights = [
+                jnp.exp2((score - top) * SCORE_SCALE).astype(jnp.bfloat16)
+                for score, top in zip(scores, tops)
+            ]
+            mixes = [
+                head_mix(weight, kv[pair, :, which * KVDIM + NOPE : (which + 1) * KVDIM])
+                for (pair, which), weight in zip(where, weights)
+            ]
+            for (pair, which), mixed in zip(where, mixes):
                 finish(pair, which, mixed)
             return carry
 
-        lax.fori_loop(0, pairs, attend, 0, unroll=2)
+        lax.fori_loop(0, 2 * pairs // together, attend, 0)
     else:
 
         def attend(pair, carry):

time: 22.3 us -> 22.1 us (level)
  the two profiles are of different devices: /device:TPU:30 before, /device:TPU:27 now
where the time goes in v6:
time: 22.1 us; the launch traced here: 21.9 us
  Pallas kernels  20.5 us (93%)
  local copies, waits for them, and re-layouts  0.8 us (4%)
  between operations  0.66 us (3%)
    pallas_call x1, Pallas kernels, per_device(): pl.pallas_call(functools.partial(kernel, n, n_head, n_sub, chunk), out_sh...  20.5 us
    unnamed x1, local copies, waits for them, and re-layouts  0.8 us

profile of v6, /device:TPU:27, one launch (start us, length us, event | category | flops | bytes accessed | tf_op | source)
XLA Modules:
  0.0 21.9 jit_solution(2395484716195965038)
XLA Ops:
  0.7 20.5 %mla_prefill.1 = bf16[128,2048]{1,0:T(8,128)(2,1)S(1)} custom-call(s32[1]{0:T(128)S(6)} %copy.9.length_ref, bf16[128,3072]{1,0:T(8,128)(2,1)} %queries.1, bf16[128,512]{1,0:T(8,128)(2,1)} %latent.1, bf16[64,128]{1,0:T(8,128)(2,1)} %bitcast.1, f32[512]{0:T(512)} %latent_gain.1, bf16[512,4096]{1,0:T(8,128)(2,1)} %up_weight.1), custom_call_target="tpu_custom_call" | custom-call | flops 2818572288 | bytes 5505024 | tf_op jit(solution)/shard_map/mla_prefill/pallas_call | solution.py:356
  21.1 0.8 %copy.8 = bf16[128,2048]{1,0:T(8,128)(2,1)} copy(bf16[128,2048]{1,0:T(8,128)(2,1)S(1)} %mla_prefill.1) | data formatting | bytes 1048576

commit v7 on v6

--- a/solution.py
+++ b/solution.py
@@ -103,6 +103,12 @@
             pl.semaphore_signal(
                 barrier, inc=1, device_id={"sub": lax.rem(sub + step, n_sub)}, device_id_type=MESH
             )
+            for h_step in range(1, n_head):
+                pl.semaphore_signal(
+                    barrier, inc=1,
+                    device_id={"head": lax.rem(head + h_step, n_head), "sub": lax.rem(sub + step, n_sub)},
+                    device_id_type=MESH,
+                )
 
     cosine, sine = angle_tables(ctx * rows, rows)
 
@@ -144,7 +150,7 @@
 
     lax.fori_loop(0, pairs, ready, 0)
 
-    waits = jnp.where(ctx > 0, n_head - 1 + n_sub - 1, 0) + (n - 1 - ctx)
+    waits = jnp.where(ctx > 0, n_head * n_sub - 1, 0) + (n - 1 - ctx)
     pl.semaphore_wait(barrier, waits)
 
     def rows_of(slot, x, s):
@@ -171,6 +177,14 @@
             device_id={"sub": lax.rem(sub + step, n_sub)}, device_id_type=MESH,
         )
 
+    def diagonal_copy(shard, h_step, step):
+        where = keys.at[rows_of(shard, head, sub)]
+        to_head = lax.rem(head + h_step, n_head)
+        return pltpu.make_async_remote_copy(
+            where, where, s_send.at[shard, to_head, step], s_recv.at[shard, head, sub],
+            device_id={"head": to_head, "sub": lax.rem(sub + step, n_sub)}, device_id_type=MESH,
+        )
+
     for target in range(n - 1, 0, -1):
 
         @pl.when(ctx < target)
@@ -182,14 +196,14 @@
             keys[block, pl.ds(0, width)], w_buf[pair], preferred_element_type=jnp.float32
         ).astype(jnp.bfloat16)
 
-    def expand(block, fresh):
+    def expand(block, first, last, fresh):
         def one(pair, carry):
             if fresh:
                 w_load(pair).wait()
             kv[pair, block, :] = project(block, pair)
             return carry
 
-        lax.fori_loop(0, pairs, one, 0, unroll=2)
+        lax.fori_loop(first, last, one, 0, unroll=2)
 
     def pass_on(shard):
         @pl.when(shard < ctx)
@@ -199,6 +213,9 @@
                 x_copy(shard, head, step).start()
             for step in range(1, n_sub):
                 s_copy(shard, head, sub, step).start()
+                if shard == 0:
+                    for h_step in range(1, n_head):
+                        diagonal_copy(shard, h_step, step).start()
 
     def pass_to_sibling(shard):
         @pl.when(shard < ctx)
@@ -206,7 +223,7 @@
             for step in range(1, n_head):
                 x = lax.rem(head + step, n_head)
                 x_copy(shard, x, step).wait_recv()
-                for s_step in range(1, n_sub):
+                for s_step in range(1, n_sub if shard else 1):
                     s_copy(shard, x, sub, s_step).start()
 
     def complete(shard):
@@ -216,15 +233,16 @@
 
     order = list(range(n - 2, -1, -1))
     if n_chunks == 1:
-        expand(own, True)
+        expand(own, 0, pairs // 2, True)
     else:
         for pair in range(pairs):
             w_load(pair).wait()
-    pass_on(order[0])
-    for earlier, later in zip(order[:-1], order[1:]):
-        pass_on(later)
-        pass_to_sibling(earlier)
-    pass_to_sibling(order[-1])
+    for shard in order:
+        pass_on(shard)
+    if n_chunks == 1:
+        expand(own, pairs // 2, pairs, True)
+    for shard in order:
+        pass_to_sibling(shard)
     for shard in order:
 
         @pl.when(shard < ctx)
@@ -263,7 +281,7 @@
     if n_chunks == 1:
         allowed = allowed_keys(0)
 
-        expand(pl.ds(0, others), False)
+        expand(pl.ds(0, others), 0, pairs, False)
         together = 4 if pairs % 2 == 0 else 2
 
         def attend(step, carry):

time: 22.1 us -> 20.9 us (0.946)
  the two profiles are of different devices: /device:TPU:27 before, /device:TPU:17 now
where the time goes in v7:
time: 20.9 us; the launch traced here: 20.8 us
  Pallas kernels  19.3 us (92%)
  local copies, waits for them, and re-layouts  0.8 us (4%)
  between operations  0.66 us (3%)
    pallas_call x1, Pallas kernels, per_device(): pl.pallas_call(functools.partial(kernel, n, n_head, n_sub, chunk), out_sh...  19.3 us
    unnamed x1, local copies, waits for them, and re-layouts  0.8 us

profile of v7, /device:TPU:17, one launch (start us, length us, event | category | flops | bytes accessed | tf_op | source)
XLA Modules:
  0.0 20.8 jit_solution(8796115611514345468)
XLA Ops:
  0.7 19.3 %mla_prefill.1 = bf16[128,2048]{1,0:T(8,128)(2,1)S(1)} custom-call(s32[1]{0:T(128)S(6)} %copy.9.length_ref, bf16[128,3072]{1,0:T(8,128)(2,1)} %queries.1, bf16[128,512]{1,0:T(8,128)(2,1)} %latent.1, bf16[64,128]{1,0:T(8,128)(2,1)} %bitcast.1, f32[512]{0:T(512)} %latent_gain.1, bf16[512,4096]{1,0:T(8,128)(2,1)} %up_weight.1), custom_call_target="tpu_custom_call" | custom-call | flops 2818572288 | bytes 5505024 | tf_op jit(solution)/shard_map/mla_prefill/pallas_call | solution.py:374
  20.0 0.8 %copy.8 = bf16[128,2048]{1,0:T(8,128)(2,1)} copy(bf16[128,2048]{1,0:T(8,128)(2,1)S(1)} %mla_prefill.1) | data formatting | bytes 1048576

commit v8 on v6

--- a/solution.py
+++ b/solution.py
@@ -182,14 +182,14 @@
             keys[block, pl.ds(0, width)], w_buf[pair], preferred_element_type=jnp.float32
         ).astype(jnp.bfloat16)
 
-    def expand(block, fresh):
+    def expand(block, first, last, fresh):
         def one(pair, carry):
             if fresh:
                 w_load(pair).wait()
             kv[pair, block, :] = project(block, pair)
             return carry
 
-        lax.fori_loop(0, pairs, one, 0, unroll=2)
+        lax.fori_loop(first, last, one, 0, unroll=4)
 
     def pass_on(shard):
         @pl.when(shard < ctx)
@@ -216,15 +216,16 @@
 
     order = list(range(n - 2, -1, -1))
     if n_chunks == 1:
-        expand(own, True)
+        expand(own, 0, pairs // 2, True)
     else:
         for pair in range(pairs):
             w_load(pair).wait()
-    pass_on(order[0])
-    for earlier, later in zip(order[:-1], order[1:]):
-        pass_on(later)
-        pass_to_sibling(earlier)
-    pass_to_sibling(order[-1])
+    for shard in order:
+        pass_on(shard)
+    if n_chunks == 1:
+        expand(own, pairs // 2, pairs, True)
+    for shard in order:
+        pass_to_sibling(shard)
     for shard in order:
 
         @pl.when(shard < ctx)
@@ -263,8 +264,8 @@
     if n_chunks == 1:
         allowed = allowed_keys(0)
 
-        expand(pl.ds(0, others), False)
-        together = 4 if pairs % 2 == 0 else 2
+        expand(pl.ds(0, others), 0, pairs, False)
+        together = 8 if pairs % 4 == 0 else 2
 
         def attend(step, carry):
             where = [(step * (together // 2) + k // 2, k % 2) for k in range(together)]

time: 22.1 us -> 20.1 us (0.910)
  the two profiles are of different devices: /device:TPU:27 before, /device:TPU:17 now
where the time goes in v8:
time: 20.1 us; the launch traced here: 20 us
  Pallas kernels  18.5 us (92%)
  local copies, waits for them, and re-layouts  0.8 us (4%)
  between operations  0.66 us (3%)
    pallas_call x1, Pallas kernels, per_device(): pl.pallas_call(functools.partial(kernel, n, n_head, n_sub, chunk), out_sh...  18.5 us
    unnamed x1, local copies, waits for them, and re-layouts  0.8 us

profile of v8, /device:TPU:17, one launch (start us, length us, event | category | flops | bytes accessed | tf_op | source)
XLA Modules:
  0.0 20.0 jit_solution(13910992684096604914)
XLA Ops:
  0.7 18.5 %mla_prefill.1 = bf16[128,2048]{1,0:T(8,128)(2,1)S(1)} custom-call(s32[1]{0:T(128)S(6)} %copy.9.length_ref, bf16[128,3072]{1,0:T(8,128)(2,1)} %queries.1, bf16[128,512]{1,0:T(8,128)(2,1)} %latent.1, bf16[64,128]{1,0:T(8,128)(2,1)} %bitcast.1, f32[512]{0:T(512)} %latent_gain.1, bf16[512,4096]{1,0:T(8,128)(2,1)} %up_weight.1), custom_call_target="tpu_custom_call" | custom-call | flops 2818572288 | bytes 5505024 | tf_op jit(solution)/shard_map/mla_prefill/pallas_call | solution.py:357
  19.2 0.8 %copy.8 = bf16[128,2048]{1,0:T(8,128)(2,1)} copy(bf16[128,2048]{1,0:T(8,128)(2,1)S(1)} %mla_prefill.1) | data formatting | bytes 1048576

commit v9 on v8

--- a/solution.py
+++ b/solution.py
@@ -119,6 +119,39 @@
     keys[own, pl.ds(0, width)] = normed
     keys[own, pl.ds(width, 2 * ROPE)] = rotated
 
+    waits = jnp.where(ctx > 0, n_head - 1 + n_sub - 1, 0) + (n - 1 - ctx)
+    pl.semaphore_wait(barrier, waits)
+
+    def rows_of(slot, x, s):
+        return pl.ds(pl.multiple_of(slot * rows + (x * n_sub + s) * piece, piece), piece)
+
+    def z_copy(shard, target):
+        return pltpu.make_async_remote_copy(
+            keys.at[rows_of(n - 1, head, sub)], keys.at[rows_of(shard, head, sub)],
+            z_send.at[target], z_recv.at[shard],
+            device_id={"ctx": target}, device_id_type=MESH,
+        )
+
+    def x_copy(shard, x, step):
+        where = keys.at[rows_of(shard, x, sub)]
+        return pltpu.make_async_remote_copy(
+            where, where, x_send.at[shard, step], x_recv.at[shard, x],
+            device_id={"head": lax.rem(head + step, n_head)}, device_id_type=MESH,
+        )
+
+    def s_copy(shard, x, s, step):
+        where = keys.at[rows_of(shard, x, s)]
+        return pltpu.make_async_remote_copy(
+            where, where, s_send.at[shard, x, step], s_recv.at[shard, x, s],
+            device_id={"sub": lax.rem(sub + step, n_sub)}, device_id_type=MESH,
+        )
+
+    for target in range(n - 1, 0, -1):
+
+        @pl.when(ctx < target)
+        def _():
+            z_copy(ctx, target).start()
+
     for slot in range(n - 1):
 
         @pl.when(ctx <= slot)
@@ -143,39 +176,6 @@
         return carry
 
     lax.fori_loop(0, pairs, ready, 0)
-
-    waits = jnp.where(ctx > 0, n_head - 1 + n_sub - 1, 0) + (n - 1 - ctx)
-    pl.semaphore_wait(barrier, waits)
-
-    def rows_of(slot, x, s):
-        return pl.ds(pl.multiple_of(slot * rows + (x * n_sub + s) * piece, piece), piece)
-
-    def z_copy(shard, target):
-        return pltpu.make_async_remote_copy(
-            keys.at[rows_of(n - 1, head, sub)], keys.at[rows_of(shard, head, sub)],
-            z_send.at[target], z_recv.at[shard],
-            device_id={"ctx": target}, device_id_type=MESH,
-        )
-
-    def x_copy(shard, x, step):
-        where = keys.at[rows_of(shard, x, sub)]
-        return pltpu.make_async_remote_copy(
-            where, where, x_send.at[shard, step], x_recv.at[shard, x],
-            device_id={"head": lax.rem(head + step, n_head)}, device_id_type=MESH,
-        )
-
-    def s_copy(shard, x, s, step):
-        where = keys.at[rows_of(shard, x, s)]
-        return pltpu.make_async_remote_copy(
-            where, where, s_send.at[shard, x, step], s_recv.at[shard, x, s],
-            device_id={"sub": lax.rem(sub + step, n_sub)}, device_id_type=MESH,
-        )
-
-    for target in range(n - 1, 0, -1):
-
-        @pl.when(ctx < target)
-        def _():
-            z_copy(ctx, target).start()
 
     def project(block, pair):
         return jnp.dot(

time: 20.1 us -> 19 us (0.945)
  Pallas kernels: 18.5 us -> 17.4 us
    pallas_call x1, Pallas kernels: 18.5 us -> 17.4 us  [per_device(): pl.pallas_call(functools.partial(kernel, n, n_head, n_sub, chunk), out_sh...]
where the time goes in v9:
time: 19 us; the launch traced here: 18.9 us
  Pallas kernels  17.4 us (92%)
  local copies, waits for them, and re-layouts  0.8 us (4%)
  between operations  0.66 us (3%)
    pallas_call x1, Pallas kernels, per_device(): pl.pallas_call(functools.partial(kernel, n, n_head, n_sub, chunk), out_sh...  17.4 us
    unnamed x1, local copies, waits for them, and re-layouts  0.8 us

profile of v9, /device:TPU:17, one launch (start us, length us, event | category | flops | bytes accessed | tf_op | source)
XLA Modules:
  0.0 18.9 jit_solution(9289769491037865765)
XLA Ops:
  0.7 17.4 %mla_prefill.1 = bf16[128,2048]{1,0:T(8,128)(2,1)S(1)} custom-call(s32[1]{0:T(128)S(6)} %copy.9.length_ref, bf16[128,3072]{1,0:T(8,128)(2,1)} %queries.1, bf16[128,512]{1,0:T(8,128)(2,1)} %latent.1, bf16[64,128]{1,0:T(8,128)(2,1)} %bitcast.1, f32[512]{0:T(512)} %latent_gain.1, bf16[512,4096]{1,0:T(8,128)(2,1)} %up_weight.1), custom_call_target="tpu_custom_call" | custom-call | flops 2818572288 | bytes 5505024 | tf_op jit(solution)/shard_map/mla_prefill/pallas_call | solution.py:357
  18.1 0.8 %copy.8 = bf16[128,2048]{1,0:T(8,128)(2,1)} copy(bf16[128,2048]{1,0:T(8,128)(2,1)S(1)} %mla_prefill.1) | data formatting | bytes 1048576
